TPU v7x, 512 devices: a whole 4x8x8 slice. The times are simulated.
512 devices in a mesh: seq: 32 (over y, x), mp: 16 (over z, core).
Axes of the slice: x: 4, y: 8, z: 8, core: 2. Of those that a mesh axis runs over, the one named last changes fastest.
Arguments:
- frames: bfloat16 [1536, 100, 232], P('seq'), may hold values from -6 to 6
- instr_ids: int32 [1536], P('seq'), may hold values from 0 to 63
- film_table: float32 [64, 2, 384], replicated, may hold values from -1.5 to 1.5
- w_expand: bfloat16 [232, 1392], P(None, 'mp'), may hold values from -0.375 to 0.375
- w_depth: float32 [9, 1392], P(None, 'mp'), may hold values from -2 to 2
- w_squeeze: float32 [1392, 58], P('mp'), may hold values from -0.625 to 0.625
- w_excite: float32 [58, 1392], P(None, 'mp'), may hold values from -3.5 to 3.5
- w_project: bfloat16 [1392, 384], P('mp'), may hold values from -0.3125 to 0.3125
- w_learner: float32 [384, 8], replicated, may hold values from -0.625 to 0.625
- token_dest: int32 [12288, 1], P('seq'), may hold values from 0 to 31; in each aligned block of 384 rows (0 to 383, 384 to 767, ...) at most 24 rows name the same one
- w_policy: bfloat16 [384, 8192], P(None, 'mp'), may hold values from -0.3125 to 0.3125
- policy_cot: bfloat16 [24576, 8192], P('seq', 'mp'), may hold values from -6 to 6
Outputs:
- policy_in: bfloat16 [24576, 8192], P('seq', 'mp')
- feature_grad: bfloat16 [1536, 100, 384], P('seq', None, 'mp')
Inputs may be any that keep to these rules, and one draw needn't show every extreme that they name: `token_dest`: within the 384 token rows of one index of seq no owner is named more than 24 times.
All inputs are finite; a program needn't handle non-finite values.
Results may differ from a plain program's by a relative error of at most 0.005.
Values may be sent and summed in bfloat16 or wider, within the bound.
No kernel may reach another device: no remote copies, remote signals or barrier semaphores. Data moves between devices by JAX's collectives and lax.ppermute only.
A program may use at most 64 MiB of HBM per device.

v0:
```python
import jax
import jax.numpy as jnp
from jax import lax
from jax.sharding import PartitionSpec as P

KS = 3
GRID = 10


highest = lax.Precision.HIGHEST


def swish(value):
    return value * jax.nn.sigmoid(value)


def depth_conv(field, kernel):
    reach = KS // 2
    side = field.shape[1]
    padded = jnp.pad(field, ((0, 0), (reach, reach), (reach, reach), (0, 0)))
    total = jnp.zeros(field.shape, jnp.float32)
    for row in range(KS):
        for col in range(KS):
            total = (
                total + kernel[row * KS + col] * padded[:, row : row + side, col : col + side, :]
            )
    return total


def per_device(
    frames,
    instr_ids,
    film_table,
    w_expand,
    w_depth,
    w_squeeze,
    w_excite,
    w_project,
    w_learner,
    token_dest,
    w_policy,
    policy_cot,
):
    count = frames.shape[0]
    cells = frames.shape[1]
    hidden_local = w_expand.shape[1]
    width = w_project.shape[1]
    n_tokens = w_learner.shape[1]
    share_width = width // lax.axis_size("mp")
    peers = lax.axis_size("seq")
    capacity = policy_cot.shape[0] // peers
    token_rows = count * n_tokens
    column = lax.axis_index("mp") * share_width
    expanded = swish(
        jnp.dot(
            frames.reshape(count * cells, frames.shape[2]),
            w_expand,
            preferred_element_type=jnp.float32,
        )
    )
    expanded = expanded.reshape(count, GRID, GRID, hidden_local)
    depthwise = swish(depth_conv(expanded, w_depth))
    squeezed = jnp.mean(depthwise, axis=(1, 2))
    reduced = lax.psum(jnp.dot(squeezed, w_squeeze, precision=highest), "mp")
    excite = jax.nn.sigmoid(jnp.dot(swish(reduced), w_excite, precision=highest))
    hidden = (
        (depthwise * excite[:, None, None, :])
        .astype(jnp.bfloat16)
        .reshape(count, cells, hidden_local)
    )
    n_instr = film_table.shape[0]
    choose = (instr_ids[:, None] == jnp.arange(n_instr, dtype=jnp.int32)[None, :]).astype(
        jnp.float32
    )
    film = jnp.dot(choose, film_table.reshape(n_instr, 2 * width), precision=highest).reshape(
        count, 2, width
    )
    scale = 1.0 + film[:, 0]
    shift = film[:, 1]
    project_wide = w_project.astype(jnp.float32)
    hidden_wide = hidden.astype(jnp.float32)
    learner_map = jnp.einsum("hc,fc,ci->fhi", project_wide, scale, w_learner, precision=highest)
    logit_part = jnp.einsum("fph,fhi->fpi", hidden_wide, learner_map, precision=highest)
    logits = lax.psum(logit_part, "mp")
    logits = logits + jnp.einsum("fc,ci->fi", shift, w_learner, precision=highest)[:, None, :]
    attend = jax.nn.sigmoid(logits)
    pooled = jnp.einsum("fpi,fph->fih", attend, hidden_wide, precision=highest) / cells
    token_part = jnp.einsum("fih,hc->fic", pooled, project_wide, precision=highest)
    weight_mean = jnp.sum(attend, axis=1) / cells
    dest = token_dest[:, 0]
    named = (dest[:, None] == jnp.arange(peers, dtype=jnp.int32)[None, :]).astype(jnp.int32)
    position = jnp.sum((jnp.cumsum(named, axis=0) - named) * named, axis=1)
    slot = dest * capacity + position
    scale_mine = lax.dynamic_slice_in_dim(scale, column, share_width, 1)
    summed = lax.psum(token_part, "mp")
    tokens = scale[:, None, :] * summed + shift[:, None, :] * weight_mean[:, :, None]
    tokens = tokens.astype(jnp.bfloat16).reshape(token_rows, width)
    outgoing = jnp.zeros((peers * capacity, width), jnp.bfloat16).at[slot].set(tokens)
    policy_in = jnp.einsum(
        "skc,cd->skd",
        lax.all_to_all(
            outgoing.reshape(peers, capacity, width), "seq", split_axis=0, concat_axis=0, tiled=True
        ),
        w_policy,
        preferred_element_type=jnp.float32,
    ).astype(jnp.bfloat16)
    policy_in = policy_in.reshape(peers * capacity, policy_in.shape[2])
    grad_part = jnp.einsum("rd,cd->rc", policy_cot, w_policy, preferred_element_type=jnp.float32)
    arrived = lax.all_to_all(
        grad_part.reshape(peers, capacity, width), "seq", split_axis=0, concat_axis=0, tiled=True
    )
    picked = arrived.reshape(peers * capacity, width)[slot]
    token_grad = lax.psum(picked, "mp")
    token_grad = token_grad.reshape(count, n_tokens, width)
    direction = jnp.einsum("hc,fc,fic->fhi", project_wide, scale, token_grad, precision=highest)
    inner_part = jnp.einsum("fph,fhi->fpi", hidden_wide, direction, precision=highest)
    inner = lax.psum(inner_part, "mp")
    inner = inner + jnp.einsum("fc,fic->fi", shift, token_grad, precision=highest)[:, None, :]
    slope = inner / cells * attend * (1.0 - attend)
    grad_mine = lax.dynamic_slice_in_dim(token_grad, column, share_width, 2)
    learner_mine = lax.dynamic_slice_in_dim(w_learner, column, share_width, 0)
    result = jnp.einsum("fpi,fic->fpc", attend, grad_mine, precision=highest) / cells
    result = result + jnp.einsum("fpi,ci->fpc", slope, learner_mine, precision=highest)
    feature_grad = (scale_mine[:, None, :] * result).astype(jnp.bfloat16)
    return (policy_in, feature_grad)


def solution(mesh):
    return jax.shard_map(
        per_device,
        mesh=mesh,
        in_specs=(
            P("seq", None, None),
            P("seq"),
            P(),
            P(None, "mp"),
            P(None, "mp"),
            P("mp", None),
            P(None, "mp"),
            P("mp", None),
            P(),
            P("seq", None),
            P(None, "mp"),
            P("seq", "mp"),
        ),
        out_specs=(P("seq", "mp"), P("seq", None, "mp")),
        check_vma=False,
    )
```

profile of v0, /device:TPU:6, one launch (start us, length us, event | category | flops | bytes accessed | tf_op | source)
XLA Modules:
  0.0 405.1 jit_solution(6442648487339237546)
XLA Ops:
  8.3 2.7 fusion.85
  11.0 10.2 %all-to-all-start.1 = ((f32[32,24,384]{2,1,0:T(8,128)}), f32[32,24,384]{2,1,0:T(8,128)S(1)}, u32[]{:S(2)}, u32[]{:S(2)}) async-start(f32[32,24,384]{2,1,0:T(8,128)} %bitcast.25), calls=%async_computation.1 | async-start | bytes 2359296 | tf_op jit(solution)/shard_map/all_to_all | solution.py:109
  21.3 4.0 copy.30
  25.3 4.3 %reshape.75 = bf16[4800,232]{1,0:T(8,128)(2,1)} reshape(bf16[48,100,232]{2,1,0:T(8,128)(2,1)} %copy.30) | data formatting | bytes 4454400 | tf_op jit(solution)/shard_map/reshape | solution.py:56
  29.7 3.8 divide_multiply_fusion.1
  33.5 3.1 copy.31
  36.5 4.2 %reshape.76 = f32[48,10,10,87]{3,2,1,0:T(8,128)} reshape(f32[4800,87]{1,0:T(8,128)} %copy.31) | data formatting | bytes 3340800 | tf_op jit(solution)/shard_map/reshape | solution.py:61
  40.7 20.0 %fusion.83 = (f32[48,87]{1,0:T(8,128)S(1)}, f32[48,10,10,87]{3,2,1,0:T(8,128)}) fusion(f32[87]{0:T(128)S(1)} %get-tuple-element.20, f32[87]{0:T(128)S(1)} %get-tuple-element.21, f32[87]{0:T(128)S(1)} %get-tuple-element.14, f32[87]{0:T(128)S(1)} %get-tuple-element.15, f32[48,10,10,87]{3,2,1,0:T(8,128)} %reshape.76, f32[87]{0:T(128)S(1)} %get-tuple-element.16, ...), kind=kLoop, calls=%fused_computation.124 | loop fusion | flops 9183024 | bytes 3360636 | tf_op jit(solution)/shard_map/reduce_sum | solution.py:63
  61.0 53.5 %psum.35 = f32[48,58]{1,0:T(8,128)S(1)} all-reduce(f32[48,58]{1,0:T(8,128)S(1)} %fusion.63), channel_id=1, replica_groups=mesh['seq'=32,'mp'=16] {'mp'}, use_global_device_ids=true, to_apply=%region_4.5 | all-reduce | flops 2784 | bytes 22272 | tf_op jit(solution)/shard_map/psum | solution.py:64
  114.6 2.6 multiply_convert_fusion
  117.3 1.5 copy.32
  118.8 2.0 copy.34
  123.5 1.7 fusion.84
  125.1 2.2 gather_fusion
  127.8 113.3 %all-reduce.8.cloned.1.call-done = (f32[48,100,8]{1,2,0:T(8,128)}, f32[48,8,384]{2,1,0:T(8,128)}) async-done(((f32[48,100,8]{1,2,0:T(8,128)}, f32[48,8,384]{2,1,0:T(8,128)}), (f32[48,100,8]{1,2,0:T(8,128)}, f32[48,8,384]{2,1,0:T(8,128)})) %all-reduce.8.cloned.1.call-update) | async-done | bytes 743440 | tf_op jit(solution)/shard_map/psum | solution.py:84
  241.1 1.5 fusion.22
  242.6 1.7 fusion.86
  244.3 2.8 convolution_multiply_fusion.1
  248.6 116.9 %all-reduce.6.cloned.1.call-done = (f32[48,8,384]{2,1,0:T(8,128)}, f32[48,100,8]{1,2,0:T(8,128)}) async-done(((f32[48,8,384]{2,1,0:T(8,128)}, f32[48,100,8]{1,2,0:T(8,128)}), (f32[48,8,384]{2,1,0:T(8,128)}, f32[48,100,8]{1,2,0:T(8,128)})) %all-reduce.6.cloned.1.call-update) | async-done | bytes 743440 | tf_op jit(solution)/shard_map/psum | solution.py:95
  365.5 3.4 scatter_custom_fusion
  368.9 9.9 %all-to-all-start = ((bf16[32,24,384]{2,1,0:T(8,128)(2,1)}), bf16[32,24,384]{2,1,0:T(8,128)(2,1)S(1)}, u32[]{:S(2)}, u32[]{:S(2)}) async-start(bf16[32,24,384]{2,1,0:T(8,128)(2,1)} %bitcast.21), calls=%async_computation | async-start | bytes 1179648 | tf_op jit(solution)/shard_map/all_to_all | solution.py:101
  381.1 2.3 convolution_multiply_fusion
  383.5 1.5 fusion.17
  385.0 11.8 %all-to-all-done = bf16[32,24,384]{2,1,0:T(8,128)(2,1)S(1)} async-done(((bf16[32,24,384]{2,1,0:T(8,128)(2,1)}), bf16[32,24,384]{2,1,0:T(8,128)(2,1)S(1)}, u32[]{:S(2)}, u32[]{:S(2)}) %all-to-all-start) | async-done | bytes 589856 | tf_op jit(solution)/shard_map/all_to_all | solution.py:101
  (56 shorter events, 9.9 us)
Async XLA Ops:
  7.2 1.1 copy-start
  7.2 14.1 %copy-start.10 = (f32[9,87]{1,0:T(8,128)S(1)}, f32[9,87]{1,0:T(8,128)}, u32[]{:S(2)}) copy-start(f32[9,87]{1,0:T(8,128)} %param.16) | copy-start | bytes 9400
  11.0 114.1 %all-to-all-start.1 = ((f32[32,24,384]{2,1,0:T(8,128)}), f32[32,24,384]{2,1,0:T(8,128)S(1)}, u32[]{:S(2)}, u32[]{:S(2)}) async-start(f32[32,24,384]{2,1,0:T(8,128)} %bitcast.25), calls=%async_computation.1 | async-start | bytes 2359296 | tf_op jit(solution)/shard_map/all_to_all | solution.py:109
  21.2 219.9 %all-reduce.8.cloned.1.call-start = ((), (), s32[]{:S(2)}) async-start(), calls=%async_computation.3 | async-start | bytes 1572864 | tf_op jit(solution)/shard_map/psum | solution.py:84
  21.3 8.4 %copy-start.13 = (bf16[232,87]{0,1:T(8,128)(2,1)S(1)}, bf16[232,87]{0,1:T(8,128)(2,1)}, u32[]{:S(2)}) copy-start(bf16[232,87]{0,1:T(8,128)(2,1)} %param.15) | copy-start | bytes 121108
  40.7 20.1 %copy-start.8 = (f32[87,58]{0,1:T(8,128)S(1)}, f32[87,58]{0,1:T(8,128)}, u32[]{:S(2)}) copy-start(f32[87,58]{0,1:T(8,128)} %param.17) | copy-start | bytes 60556
  40.7 73.7 %copy-start.14 = (f32[58,87]{1,0:T(8,128)S(1)}, f32[58,87]{1,0:T(8,128)}, u32[]{:S(2)}) copy-start(f32[58,87]{1,0:T(8,128)} %param.18) | copy-start | bytes 60556
  117.2 3.6 copy-start.9
  117.2 4.9 %copy-start.4 = (f32[64,2,384]{2,1,0:T(2,128)S(1)}, f32[64,2,384]{2,1,0:T(2,128)}, u32[]{:S(2)}) copy-start(f32[64,2,384]{2,1,0:T(2,128)} %param.14) | copy-start | bytes 589828
  117.2 4.9 %copy-start.11 = (s32[48]{0:T(128)S(1)}, s32[48]{0:T(128)}, u32[]{:S(2)}) copy-start(s32[48]{0:T(128)} %param.13) | copy-start | bytes 580
  117.2 5.8 %copy-start.3 = (bf16[87,384]{1,0:T(8,128)(2,1)S(1)}, bf16[87,384]{1,0:T(8,128)(2,1)}, u32[]{:S(2)}) copy-start(bf16[87,384]{1,0:T(8,128)(2,1)} %param.19) | copy-start | bytes 200452
  117.2 5.8 %copy-start.7 = (f32[384,8]{0,1:T(8,128)S(1)}, f32[384,8]{0,1:T(8,128)}, u32[]{:S(2)}) copy-start(f32[384,8]{0,1:T(8,128)} %param.20) | copy-start | bytes 36868
  127.4 238.1 %all-reduce.6.cloned.1.call-start = ((), (), s32[]{:S(2)}) async-start(), calls=%async_computation.2 | async-start | bytes 1572864 | tf_op jit(solution)/shard_map/psum | solution.py:95
  241.1 7.2 %copy-start.5 = (f32[48,100,8]{1,2,0:T(8,128)S(1)}, f32[48,100,8]{1,2,0:T(8,128)}, u32[]{:S(2)}) copy-start(f32[48,100,8]{1,2,0:T(8,128)} %get-tuple-element.4) | copy-start | bytes 460804
  242.6 137.0 %copy-start.1 = (f32[48,8,384]{2,1,0:T(8,128)S(1)}, f32[48,8,384]{2,1,0:T(8,128)}, u32[]{:S(2)}) copy-start(f32[48,8,384]{2,1,0:T(8,128)} %get-tuple-element.5) | copy-start | bytes 1769476
  247.1 136.4 %copy-start.6 = (f32[48,100,8]{1,2,0:T(8,128)S(1)}, f32[48,100,8]{1,2,0:T(8,128)}, u32[]{:S(2)}) copy-start(f32[48,100,8]{1,2,0:T(8,128)} %get-tuple-element.4) | copy-start | bytes 460804
  247.1 149.7 %copy-start.2 = (bf16[384,512]{1,0:T(8,128)(2,1)S(1)}, bf16[384,512]{1,0:T(8,128)(2,1)}, u32[]{:S(2)}) copy-start(bf16[384,512]{1,0:T(8,128)(2,1)} %param.22) | copy-start | bytes 1179652
  365.5 18.0 %copy-start.12 = (f32[48,100,8]{1,2,0:T(8,128)S(1)}, f32[48,100,8]{1,2,0:T(8,128)}, u32[]{:S(2)}) copy-start(f32[48,100,8]{1,2,0:T(8,128)} %get-tuple-element.3) | copy-start | bytes 460804
  368.9 28.0 %all-to-all-start = ((bf16[32,24,384]{2,1,0:T(8,128)(2,1)}), bf16[32,24,384]{2,1,0:T(8,128)(2,1)S(1)}, u32[]{:S(2)}, u32[]{:S(2)}) async-start(bf16[32,24,384]{2,1,0:T(8,128)(2,1)} %bitcast.21), calls=%async_computation | async-start | bytes 1179648 | tf_op jit(solution)/shard_map/all_to_all | solution.py:101
Sparse Core Ops, SparseCore 0:
  127.5 113.5 all-reduce.7
  248.4 116.9 all-reduce.5
where the time goes:
time: 406 us; the launch traced here: 405 us
  waiting for transfers between devices  242 us (60%)
  blocking collectives  53.5 us (13%)
  other arithmetic  28 us (7%)
  local copies, waits for them, and re-layouts  23.6 us (6%)
  matrix products  23.4 us (6%)
  starting transfers between devices  20.3 us (5%)
  between operations  14.3 us (4%)
    psum x1, waiting for transfers between devices, per_device(): summed = lax.psum(token_part, 'mp')  117 us
    psum x1, waiting for transfers between devices, per_device(): logits = lax.psum(logit_part, 'mp')  113 us
    psum x1, blocking collectives, per_device(): reduced = lax.psum(jnp.dot(squeezed, w_squeeze, precision=highest), 'mp')  53.5 us
    reduce_sum x1, other arithmetic, per_device(): squeezed = jnp.mean(depthwise, axis=(1, 2))  20 us
    all_to_all x1, waiting for transfers between devices, per_device(): lax.all_to_all(outgoing.reshape(peers, capacity, width), 'seq', split_axi...  11.8 us
    all_to_all x1, starting transfers between devices, per_device(): lax.all_to_all(grad_part.reshape(peers, capacity, width), 'seq', split_ax...  10.2 us
    all_to_all x1, starting transfers between devices, per_device(): lax.all_to_all(outgoing.reshape(peers, capacity, width), 'seq', split_axi...  9.86 us
  transfers between devices with their start and end apart: 4, of which 3 were waited for; matrix products, arithmetic and copies ran while one was open for 14% of the time, Pallas kernels for 0%

commit v1 on v0

v1 whole, which is shorter than its diff:
```python
import functools

import jax
import jax.numpy as jnp
from jax import lax
from jax.experimental import pallas as pl
from jax.experimental.pallas import tpu as pltpu
from jax.sharding import PartitionSpec as P

KS = 3
GRID = 10
BAND = 32
SHARD = 96
LANES = 768
TAIL = 512
MIB = 1024 * 1024

highest = lax.Precision.HIGHEST
f32 = jnp.float32
bf16 = jnp.bfloat16

NN = (((1,), (0,)), ((), ()))
NT = (((1,), (1,)), ((), ()))
TN = (((0,), (0,)), ((), ()))


def dot(a, b, dims=NN, precision=None):
    return lax.dot_general(a, b, dims, precision=precision, preferred_element_type=f32)


def sigmoid(value):
    return 0.5 + 0.5 * jnp.tanh(0.5 * value)


def swish(value):
    half = 0.5 * value
    return half + half * jnp.tanh(half)


def iota(shape, dim):
    return lax.broadcasted_iota(jnp.int32, shape, dim)


def onehot(condition, dtype=bf16):
    return jnp.where(condition, 1.0, 0.0).astype(dtype)


def halves(value):
    top = value.astype(bf16)
    return top, (value - top.astype(f32)).astype(bf16)


def call(kernel, out_shape, *args, in_specs=None, scratch=(), flops=1e6, moved=1e6, vmem=48):
    return pl.pallas_call(
        kernel,
        out_shape=out_shape,
        in_specs=in_specs or [pl.BlockSpec(memory_space=pltpu.VMEM)] * len(args),
        out_specs=jax.tree.map(lambda _: pl.BlockSpec(memory_space=pltpu.VMEM), out_shape),
        scratch_shapes=scratch,
        compiler_params=pltpu.CompilerParams(vmem_limit_bytes=vmem * MIB),
        cost_estimate=pl.CostEstimate(
            flops=int(flops), bytes_accessed=int(moved), transcendentals=0
        ),
    )(*args)


def lane_plan(width, c_in, c_se):
    exp = width
    sq = exp + c_in
    ex = sq + c_se
    dep = ex + c_se
    return exp, sq - TAIL, ex - TAIL, dep - TAIL


def pack_kernel(plan, expand, project, squeeze, excite, depth, out):
    exp, sq, ex, dep = plan
    rows, width = project.shape
    c_in = expand.shape[1]
    span = LANES - TAIL
    out[...] = jnp.zeros(out.shape, bf16)
    out[0:rows, 0:width] = project[...]
    head = TAIL - exp
    out[0:rows, exp:TAIL] = expand[:, 0:head]

    def place(value, first):
        count = value.shape[0]
        spot = onehot(iota((count, span), 1) == iota((count, span), 0) + first)
        return dot(value, spot, TN)

    top, low = halves(depth[...])
    tail = place(squeeze[...].astype(bf16), sq)
    tail = tail + place(excite[...].astype(bf16), ex)
    tail = tail + place(top, dep) + place(low, dep + KS * KS)
    rest = c_in - head
    spot = onehot(iota((c_in, span), 0) == iota((c_in, span), 1) + head)
    tail = tail + dot(expand[...], spot)
    del rest
    out[0:rows, TAIL:LANES] = tail.astype(bf16)


def trunk_kernel(
    plan, n_tokens,
    ids, cells_ref, film, learner, w,
    tokens_out, mixed_out, attend_out, scale_out,
    e, d, h, wd, exw,
):
    exp, sq, ex, dep = plan
    width = film.shape[2]
    hidden = w.shape[0]
    bands = GRID
    rows = bands * BAND
    n_frames = 3
    first = lax.axis_index("mp") * n_frames
    scales, shifts = [], []
    for f in range(n_frames):
        name = ids[first + f]
        row = film[name]
        scales.append(1.0 + row[0:1, :])
        shifts.append(row[1:2, :])

    def by_band(parts):
        frame = iota((BAND, parts[0].shape[1]), 0) % n_frames
        return jnp.where(frame == 0, parts[0], jnp.where(frame == 1, parts[1], parts[2]))

    scale_band = by_band(scales)
    shift_band = by_band(shifts)
    scale_out[...] = jnp.concatenate(scales + [jnp.zeros((8 - n_frames, width), f32)], axis=0)
    pick = (iota((16, LANES - TAIL), 1) == iota((16, LANES - TAIL), 0) + dep) | (
        iota((16, LANES - TAIL), 1) == iota((16, LANES - TAIL), 0) + dep + KS * KS
    )
    pick = onehot(pick & (iota((16, LANES - TAIL), 0) < KS * KS))
    wd[...] = dot(pick, w[:, TAIL:LANES], NT)
    e[...] = dot(cells_ref[...], w[:, exp:exp + 256], NT)
    place = iota((BAND, 128), 0)
    has_left = place >= n_frames
    has_right = place < BAND - 2 - n_frames

    def chunk(j, carry):
        lanes = pl.ds(pl.multiple_of(j * 128, 128), 128)
        taps = [wd[t:t + 1, lanes] for t in range(KS * KS)]
        total = None
        done = None
        now = None

        def finish(r, value, total):
            out = swish(value)
            d[r * BAND:(r + 1) * BAND, lanes] = out
            return out if total is None else total + out

        for r in range(bands):
            mid = swish(e[r * BAND:(r + 1) * BAND, lanes])
            left = jnp.where(has_left, pltpu.roll(mid, n_frames, 0), 0.0)
            right = jnp.where(has_right, pltpu.roll(mid, BAND - n_frames, 0), 0.0)

            def taken(row):
                return (
                    taps[row * KS] * left + taps[row * KS + 1] * mid + taps[row * KS + 2] * right
                )

            if done is not None:
                total = finish(r - 1, done + taken(2), total)
            here = taken(1)
            if now is not None:
                here = here + now
            done, now = here, taken(0)
        total = finish(bands - 1, done, total)
        exw[:, lanes] = total
        return carry

    lax.fori_loop(0, hidden // 128, chunk, 0)
    member = (iota((8, BAND), 1) % n_frames == iota((8, BAND), 0)) & (
        iota((8, BAND), 1) < BAND - 2
    )
    mean = dot(onehot(member, f32), exw[...], precision=highest) * (1.0 / (GRID * GRID))
    top, low = halves(mean)
    both = dot(jnp.concatenate([top, low], axis=0), w[:, TAIL:LANES])
    reduced = both[0:8] + both[8:16]
    turned = pltpu.roll(swish(reduced), ex - sq, 1)
    lane = iota(turned.shape, 1)
    turned = jnp.where((lane >= ex) & (lane < dep), turned, 0.0)
    top, low = halves(turned)
    both = dot(jnp.concatenate([top, low], axis=0), w[:, TAIL:LANES], NT)
    excite = sigmoid(both[0:8] + both[8:16])
    exw[...] = by_band([excite[f:f + 1] for f in range(n_frames)])
    for r in range(bands):
        part = slice(r * BAND, (r + 1) * BAND)
        h[part, :] = (d[part, :] * exw[...]).astype(bf16)
    block = dot(h[...], w[:, 0:width])
    mixed = (
        block.reshape(bands, BAND, width) * scale_band[None] + shift_band[None]
    ).reshape(rows, width)
    mixed_out[...] = mixed
    tiled = jnp.concatenate([learner[...]] * n_frames, axis=0)
    logits = dot(tiled, mixed, NT, highest)
    at = iota(logits.shape, 1) % BAND
    mine = (at % n_frames == iota(logits.shape, 0) // n_tokens) & (at < BAND - 2)
    attend = jnp.where(mine, sigmoid(logits), 0.0)
    attend_out[...] = attend
    tokens = dot(attend, mixed, precision=highest) * (1.0 / (GRID * GRID))
    tokens_out[...] = tokens.astype(bf16)


def slots_onehot(dest, peers, capacity):
    count = dest.shape[1]
    named = iota((peers, count), 0) == dest
    before = onehot(iota((count, count), 0) < iota((count, count), 1))
    ahead = dot(onehot(named), before)
    place = jnp.sum(jnp.where(named, ahead, 0.0), axis=0, keepdims=True)
    slot = dest * capacity + place.astype(jnp.int32)
    return onehot(iota((peers * capacity, count), 0) == slot)


def scatter_kernel(peers, capacity, tokens, dest, out):
    out[...] = dot(slots_onehot(dest[...], peers, capacity), tokens[...]).astype(bf16)


def pick_kernel(peers, capacity, arrived, dest, out):
    chosen = dot(slots_onehot(dest[...], peers, capacity), arrived[...], TN)
    each = out.shape[1]
    for k in range(out.shape[0]):
        out[k] = chosen[k * each:(k + 1) * each].astype(bf16)


def backward_kernel(n_tokens, mixed, attend, scale, learner, grads, out):
    n_frames = 3
    parts, _, share, cells = out.shape
    grad = grads[0].astype(f32)
    for k in range(1, grads.shape[0]):
        grad = grad + grads[k].astype(f32)
    inner = dot(grad, mixed[...], NT, highest)
    held = attend[...]
    slope = inner * (1.0 / (GRID * GRID)) * held * (1.0 - held)
    both = jnp.concatenate([held * (1.0 / (GRID * GRID)), slope], axis=0)
    shape = (mixed.shape[0], n_frames * 128)
    row, lane = iota(shape, 0), iota(shape, 1)
    cell, frame = lane % 128, lane // 128
    spot = (row == cell // GRID * BAND + cell % GRID * n_frames + frame) & (cell < cells)
    both = dot(both, onehot(spot, f32), precision=highest)
    factors = jnp.concatenate([grad] + [learner[...]] * n_frames, axis=0)
    for f in range(n_frames):
        result = dot(
            factors * scale[f:f + 1, :], both[:, f * 128:(f + 1) * 128], TN, highest
        )
        for k in range(parts):
            out[k, f] = result[k * share:(k + 1) * share, 0:cells].astype(bf16)


def per_device(
    frames,
    instr_ids,
    film_table,
    w_expand,
    w_depth,
    w_squeeze,
    w_excite,
    w_project,
    w_learner,
    token_dest,
    w_policy,
    policy_cot,
):
    count, cells, c_in = frames.shape
    width = w_project.shape[1]
    n_tokens = w_learner.shape[1]
    n_mp = lax.axis_size("mp")
    peers = lax.axis_size("seq")
    capacity = policy_cot.shape[0] // peers
    share = width // n_mp
    n_frames = count // n_mp
    c_se = w_squeeze.shape[1]
    rows = GRID * BAND
    hidden = n_mp * SHARD
    plan = lane_plan(width, c_in, c_se)
    sds = jax.ShapeDtypeStruct
    vmem = pl.BlockSpec(memory_space=pltpu.VMEM)
    dest = token_dest.T
    learner = w_learner.T

    mine = call(
        functools.partial(pack_kernel, plan),
        sds((SHARD, LANES), bf16),
        w_expand.T, w_project, w_squeeze.T, w_excite, w_depth,
    )
    packed = lax.all_gather(mine, "mp", axis=0, tiled=True)

    grad_part = dot(policy_cot, w_policy, NT).astype(bf16)
    arrived = lax.all_to_all(
        grad_part.reshape(peers, capacity, width), "seq", split_axis=0, concat_axis=0, tiled=True
    )
    picked = call(
        functools.partial(pick_kernel, peers, capacity),
        sds((n_mp, n_frames * n_tokens, width), bf16),
        arrived.reshape(peers * capacity, width), dest,
        flops=3e8, moved=2e6,
    )
    grads = lax.all_to_all(picked, "mp", split_axis=0, concat_axis=0, tiled=True)

    own = lax.dynamic_slice_in_dim(frames, lax.axis_index("mp") * n_frames, n_frames, 0)
    own = own.transpose(1, 0, 2).reshape(GRID, GRID * n_frames, c_in)
    own = jnp.pad(own, ((0, 0), (0, BAND - GRID * n_frames), (0, 256 - c_in)))
    own = own.reshape(rows, 256)
    mine, mixed, attend, scale = call(
        functools.partial(trunk_kernel, plan, n_tokens),
        (
            sds((n_frames * n_tokens, width), bf16),
            sds((rows, width), f32),
            sds((n_frames * n_tokens, rows), f32),
            sds((8, width), f32),
        ),
        instr_ids, own, film_table, learner, packed,
        in_specs=[pl.BlockSpec(memory_space=pltpu.SMEM)] + [vmem] * 4,
        scratch=[
            pltpu.VMEM((rows, hidden), f32),
            pltpu.VMEM((rows, hidden), f32),
            pltpu.VMEM((rows, hidden), bf16),
            pltpu.VMEM((16, hidden), f32),
            pltpu.VMEM((BAND, hidden), f32),
        ],
        flops=2e9, moved=3e7,
    )
    tokens = lax.all_gather(mine, "mp", axis=0, tiled=True)
    outgoing = call(
        functools.partial(scatter_kernel, peers, capacity),
        sds((peers * capacity, width), bf16),
        tokens, dest,
        flops=3e8, moved=2e6,
    )
    rows_in = lax.all_to_all(
        outgoing.reshape(peers, capacity, width), "seq", split_axis=0, concat_axis=0, tiled=True
    )
    policy_in = dot(rows_in.reshape(peers * capacity, width), w_policy).astype(bf16)

    parts = call(
        functools.partial(backward_kernel, n_tokens),
        sds((n_mp, n_frames, share, cells), bf16),
        mixed, attend, scale, learner, grads,
        flops=1e9, moved=2e6,
    )
    parts = lax.all_to_all(parts, "mp", split_axis=0, concat_axis=0, tiled=True)
    feature_grad = parts.reshape(count, share, cells).transpose(0, 2, 1)
    return (policy_in, feature_grad)


def solution(mesh):
    return jax.shard_map(
        per_device,
        mesh=mesh,
        in_specs=(
            P("seq", None, None),
            P("seq"),
            P(),
            P(None, "mp"),
            P(None, "mp"),
            P("mp", None),
            P(None, "mp"),
            P("mp", None),
            P(),
            P("seq", None),
            P(None, "mp"),
            P("seq", "mp"),
        ),
        out_specs=(P("seq", "mp"), P("seq", None, "mp")),
        check_vma=False,
    )
```

time: 406 us -> 143 us (0.35)
  waiting for transfers between devices: 242 us -> 24.4 us
  other arithmetic: 28 us -> 0 us
  matrix products: 23.4 us -> 3.27 us
  local copies, waits for them, and re-layouts: 23.6 us -> 10.3 us
  Pallas kernels: 0 us -> 12.1 us
  starting transfers between devices: 20.3 us -> 28.1 us
    psum x2 -> x0, waiting for transfers between devices: 230 us -> none  [the longest x1 117 us: per_device(): summed = lax.psum(token_part, 'mp')]
    psum x1 -> x0, blocking collectives: 53.5 us -> none  [per_device(): reduced = lax.psum(jnp.dot(squeezed, w_squeeze, precision=highest), 'mp')]
    all_to_all x0 -> x1, blocking collectives: none -> 28.4 us  [per_device(): lax.all_to_all(grad_part.reshape(peers, capacity, width), 'seq', split_ax...]
    all_gather x0 -> x1, blocking collectives: none -> 21.5 us  [per_device(): tokens = lax.all_gather(mine, 'mp', axis=0, tiled=True)]
    reduce_sum x3 -> x0, other arithmetic: 20.4 us -> none  [the longest x1 20 us: per_device(): squeezed = jnp.mean(depthwise, axis=(1, 2))]
    dot_general x16 -> x2, matrix products: 23.4 us -> 3.27 us  [dot(): lax.dot_general(a, b, dims, precision=precision, preferred_element_type=f32)]
    pallas_call x0 -> x5, Pallas kernels: none -> 12.1 us  [call(): pl.pallas_call(kernel, out_shape=out_shape, in_specs=in_specs or [pl.Bloc...]
    reshape x3 -> x1, local copies, waits for them, and re-layouts: 10.5 us -> 0.13 us  [per_device(): own = own.transpose(1, 0, 2).reshape(GRID, GRID * n_frames, c_in)]
  transfers between devices with their start and end apart: 4 -> 4, of which waited for: 3 -> 2; matrix products, arithmetic and copies ran while one was open for 14% -> 2% of each run, Pallas kernels for 0% -> 6%
where the time goes in v1:
time: 143 us; the launch traced here: 142 us
  blocking collectives  49.9 us (35%)
  starting transfers between devices  28.1 us (20%)
  waiting for transfers between devices  24.4 us (17%)
  between operations  14.2 us (10%)
  Pallas kernels  12.1 us (8%)
  local copies, waits for them, and re-layouts  10.3 us (7%)
  matrix products  3.27 us (2%)
    all_to_all x1, blocking collectives, per_device(): lax.all_to_all(grad_part.reshape(peers, capacity, width), 'seq', split_ax...  28.4 us
    all_gather x1, blocking collectives, per_device(): tokens = lax.all_gather(mine, 'mp', axis=0, tiled=True)  21.5 us
    all_to_all x1, waiting for transfers between devices, per_device(): lax.all_to_all(outgoing.reshape(peers, capacity, width), 'seq', split_axi...  18.7 us
    all_to_all x1, starting transfers between devices, per_device(): lax.all_to_all(outgoing.reshape(peers, capacity, width), 'seq', split_axi...  12.3 us
    pallas_call x5, Pallas kernels, call(): pl.pallas_call(kernel, out_shape=out_shape, in_specs=in_specs or [pl.Bloc...  12.1 us
    all_to_all x1, starting transfers between devices, per_device(): lax.all_to_all(picked, 'mp', split_axis=0, concat_axis=0, tiled=True)  10.4 us
    unnamed x31, local copies, waits for them, and re-layouts  9.96 us
    all_gather x1, waiting for transfers between devices, per_device(): packed = lax.all_gather(mine, 'mp', axis=0, tiled=True)  5.61 us
  transfers between devices with their start and end apart: 4, of which 2 were waited for; matrix products, arithmetic and copies ran while one was open for 2% of the time, Pallas kernels for 6%

profile of v1, /device:TPU:6, one launch (start us, length us, event | category | flops | bytes accessed | tf_op | source)
XLA Modules:
  0.0 142.1 jit_solution(15745429418230375367)
XLA Ops:
  7.2 1.0 copy-done.1
  8.3 0.8 copy-done.2
  9.1 0.8 copy-done.3
  9.8 0.8 copy-done.4
  10.6 0.7 copy-done.5
  11.3 0.9 shard_map.131
  12.2 1.8 %convolution_convert_fusion.1 = bf16[768,384]{1,0:T(8,128)(2,1)S(1)} fusion(bf16[768,512]{1,0:T(8,128)(2,1)} %param.23, bf16[384,512]{1,0:T(8,128)(2,1)} %param.22), kind=kOutput, calls=%fused_computation.1 | convolution fusion | flops 302284800 | bytes 1769472 | tf_op jit(solution)/shard_map/dot_general | solution.py:28
  14.1 28.4 %all_to_all.20 = bf16[32,24,384]{2,1,0:T(8,128)(2,1)S(1)} all-to-all(bf16[32,24,384]{2,1,0:T(8,128)(2,1)S(1)} %bitcast.27), channel_id=1, replica_groups=mesh['seq'=32,'mp'=16] {'seq'}, dimensions={0} | all-to-all | bytes 1179648 | tf_op jit(solution)/shard_map/all_to_all | solution.py:287
  42.4 1.4 shard_map.134
  43.8 10.4 %all-to-all-start.2 = ((bf16[16,24,384]{2,1,0:T(8,128)(2,1)}), bf16[16,24,384]{2,1,0:T(8,128)(2,1)S(1)}, u32[]{:S(2)}, u32[]{:S(2)}) async-start(bf16[16,24,384]{2,1,0:T(8,128)(2,1)} %shard_map.134), calls=%async_computation.2 | async-start | bytes 589824 | tf_op jit(solution)/shard_map/all_to_all | solution.py:296
  54.6 5.6 %all-gather.2.cloned.1.call-done.w = bf16[1536,768]{1,0:T(8,128)(2,1)} async-done(((bf16[96,768]{1,0:T(8,128)(2,1)}), bf16[1536,768]{1,0:T(8,128)(2,1)}) %all-gather.2.cloned.1.call-update) | async-done | bytes 2359312 | tf_op jit(solution)/shard_map/all_gather | solution.py:284
  60.2 1.7 %copy-done.6 = bf16[1536,768]{1,0:T(8,128)(2,1)S(1)} copy-done((bf16[1536,768]{1,0:T(8,128)(2,1)S(1)}, bf16[1536,768]{1,0:T(8,128)(2,1)}, u32[]{:S(2)}) %copy-start.6) | copy-done | bytes 2359320
  61.9 5.8 %shard_map.132 = (bf16[24,384]{1,0:T(8,128)(2,1)S(1)}, f32[320,384]{1,0:T(8,128)S(1)}, f32[24,320]{1,0:T(8,128)S(1)}, f32[8,384]{1,0:T(8,128)S(1)}) custom-call(s32[48]{0:T(128)S(1)} %copy-done.10, bf16[320,256]{1,0:T(8,128)(2,1)S(1)} %bitcast.19, f32[64,2,384]{2,1,0:T(2,128)S(1)} %copy-done.7, f32[8,384]{1,0:T(8,128)S(1)} %bitcast.22, ...), custom_call_target="tpu_custom_call" | custom-call | flops 2000000000 | bytes 30000000 | tf_op jit(solution)/shard_map/pallas_call | solution.py:54
  67.7 0.8 copy-done.11
  68.5 1.0 copy-done.12
  69.6 2.4 %shard_map.135 = bf16[16,3,24,100]{3,2,1,0:T(8,128)(2,1)} custom-call(f32[320,384]{1,0:T(8,128)S(1)} %copy-done.12, f32[24,320]{1,0:T(8,128)S(1)} %get-tuple-element.8.attend, f32[8,384]{1,0:T(8,128)S(1)} %get-tuple-element.9.scale, f32[8,384]{1,0:T(8,128)S(1)} %bitcast.23, bf16[16,24,384]{2,1,0:T(8,128)(2,1)S(1)} %all-to-all-done.2.grads), custom_call_target="tpu_custom_call" | custom-call | flops 1000000000 | bytes 2000000 | tf_op jit(solution)/shard_map/pallas_call | solution.py:54
  72.0 5.3 %all-to-all-start.3 = ((bf16[16,3,24,100]{3,2,1,0:T(8,128)(2,1)}), bf16[16,3,24,100]{3,2,1,0:T(8,128)(2,1)S(1)}, u32[]{:S(2)}, u32[]{:S(2)}) async-start(bf16[16,3,24,100]{3,2,1,0:T(8,128)(2,1)} %shard_map.135), calls=%async_computation.3 | async-start | bytes 589824 | tf_op jit(solution)/shard_map/all_to_all | solution.py:339
  77.3 21.5 %all_gather.7.tokens = bf16[384,384]{1,0:T(8,128)(2,1)S(1)} all-gather(bf16[24,384]{1,0:T(8,128)(2,1)S(1)} %get-tuple-element.6), channel_id=1, replica_groups=mesh['seq'=32,'mp'=16] {'mp'}, dimensions={0}, use_global_device_ids=true | all-gather | bytes 313344 | tf_op jit(solution)/shard_map/all_gather | solution.py:321
  98.8 1.5 %shard_map.133 = bf16[768,384]{1,0:T(8,128)(2,1)} custom-call(bf16[384,384]{1,0:T(8,128)(2,1)S(1)} %all_gather.7.tokens, s32[1,384]{1,0:T(1,128)S(1)} %bitcast.25), custom_call_target="tpu_custom_call" | custom-call | flops 300000000 | bytes 2000000 | tf_op jit(solution)/shard_map/pallas_call | solution.py:54
  100.3 0.7 copy-done.14
  101.0 12.3 %all-to-all-start = ((bf16[32,24,384]{2,1,0:T(8,128)(2,1)}), bf16[32,24,384]{2,1,0:T(8,128)(2,1)S(1)}, u32[]{:S(2)}, u32[]{:S(2)}) async-start(bf16[32,24,384]{2,1,0:T(8,128)(2,1)} %bitcast.6), calls=%async_computation | async-start | bytes 1179648 | tf_op jit(solution)/shard_map/all_to_all | solution.py:328
  113.4 18.7 %all-to-all-done = bf16[32,24,384]{2,1,0:T(8,128)(2,1)S(1)} async-done(((bf16[32,24,384]{2,1,0:T(8,128)(2,1)}), bf16[32,24,384]{2,1,0:T(8,128)(2,1)S(1)}, u32[]{:S(2)}, u32[]{:S(2)}) %all-to-all-start) | async-done | bytes 589856 | tf_op jit(solution)/shard_map/all_to_all | solution.py:328
  132.1 1.4 %convolution_convert_fusion = bf16[768,512]{1,0:T(8,128)(2,1)} fusion(bf16[768,384]{1,0:T(8,128)(2,1)S(1)} %bitcast.26, bf16[384,512]{1,0:T(8,128)(2,1)S(1)} %copy-done.13), kind=kOutput, calls=%fused_computation | convolution fusion | flops 302383104 | bytes 1769472 | tf_op jit(solution)/shard_map/dot_general | solution.py:28
  133.5 1.7 %copy.15 = bf16[48,100,24]{1,2,0:T(8,128)(2,1)} copy(bf16[48,100,24]{1,2,0:T(8,128)(2,1)} %bitcast.28) | data formatting | bytes 460800
  (28 shorter events, 0.4 us)
Async XLA Ops:
  7.2 47.1 %copy-start = (bf16[48,100,232]{2,0,1:T(8,128)(2,1)S(1)}, bf16[48,100,232]{2,0,1:T(8,128)(2,1)}, u32[]{:S(2)}) copy-start(bf16[48,100,232]{2,0,1:T(8,128)(2,1)} %param.12) | copy-start | bytes 6681604
  7.2 35.3 %copy-start.9 = (s32[384,1]{0,1:T(1,128)S(1)}, s32[384,1]{0,1:T(1,128)}, u32[]{:S(2)}) copy-start(s32[384,1]{0,1:T(1,128)} %param.21) | copy-start | bytes 4612
  7.2 53.0 %all-gather.2.cloned.1.call-start = ((), (), s32[]{:S(2)}) async-start(), calls=%async_computation.4 | async-start | bytes 2506752 | tf_op jit(solution)/shard_map/all_gather | solution.py:284
  7.2 1.0 copy-start.1
  8.3 0.8 copy-start.2
  9.1 0.8 copy-start.3
  9.8 0.8 copy-start.4
  10.6 0.7 copy-start.5
  14.0 46.2 %copy-start.7 = (f32[64,2,384]{2,1,0:T(2,128)S(1)}, f32[64,2,384]{2,1,0:T(2,128)}, u32[]{:S(2)}) copy-start(f32[64,2,384]{2,1,0:T(2,128)} %film.1) | copy-start | bytes 589828
  14.1 46.2 %copy-start.8 = (f32[384,8]{0,1:T(8,128)S(1)}, f32[384,8]{0,1:T(8,128)}, u32[]{:S(2)}) copy-start(f32[384,8]{0,1:T(8,128)} %param.20) | copy-start | bytes 36868
  14.1 46.2 %copy-start.10 = (s32[48]{0:T(128)S(1)}, s32[48]{0:T(128)}, u32[]{:S(2)}) copy-start(s32[48]{0:T(128)} %ids.1) | copy-start | bytes 580
  43.8 24.7 %all-to-all-start.2 = ((bf16[16,24,384]{2,1,0:T(8,128)(2,1)}), bf16[16,24,384]{2,1,0:T(8,128)(2,1)S(1)}, u32[]{:S(2)}, u32[]{:S(2)}) async-start(bf16[16,24,384]{2,1,0:T(8,128)(2,1)} %shard_map.134), calls=%async_computation.2 | async-start | bytes 589824 | tf_op jit(solution)/shard_map/all_to_all | solution.py:296
  60.2 1.7 %copy-start.6 = (bf16[1536,768]{1,0:T(8,128)(2,1)S(1)}, bf16[1536,768]{1,0:T(8,128)(2,1)}, u32[]{:S(2)}) copy-start(bf16[1536,768]{1,0:T(8,128)(2,1)} %all-gather.2.cloned.1.call-done.w) | copy-start | bytes 7077892
  67.7 0.8 copy-start.11
  68.5 1.0 copy-start.12
  72.0 60.1 %copy-start.13 = (bf16[384,512]{1,0:T(8,128)(2,1)S(1)}, bf16[384,512]{1,0:T(8,128)(2,1)}, u32[]{:S(2)}) copy-start(bf16[384,512]{1,0:T(8,128)(2,1)} %param.22) | copy-start | bytes 1179652
  72.0 28.4 %all-to-all-start.3 = ((bf16[16,3,24,100]{3,2,1,0:T(8,128)(2,1)}), bf16[16,3,24,100]{3,2,1,0:T(8,128)(2,1)S(1)}, u32[]{:S(2)}, u32[]{:S(2)}) async-start(bf16[16,3,24,100]{3,2,1,0:T(8,128)(2,1)} %shard_map.135), calls=%async_computation.3 | async-start | bytes 589824 | tf_op jit(solution)/shard_map/all_to_all | solution.py:339
  100.3 0.7 copy-start.14
  101.0 31.1 %all-to-all-start = ((bf16[32,24,384]{2,1,0:T(8,128)(2,1)}), bf16[32,24,384]{2,1,0:T(8,128)(2,1)S(1)}, u32[]{:S(2)}, u32[]{:S(2)}) async-start(bf16[32,24,384]{2,1,0:T(8,128)(2,1)} %bitcast.6), calls=%async_computation | async-start | bytes 1179648 | tf_op jit(solution)/shard_map/all_to_all | solution.py:328
Sparse Core Ops, SparseCore 0:
  12.3 47.8 all-gather.1

commit v2 on v1

--- a/solution.py
+++ b/solution.py
@@ -50,7 +50,7 @@
     return top, (value - top.astype(f32)).astype(bf16)
 
 
-def call(kernel, out_shape, *args, in_specs=None, scratch=(), flops=1e6, moved=1e6, vmem=48):
+def call(kernel, out_shape, *args, in_specs=None, scratch=(), flops=1e6, moved=1e6, vmem=12):
     return pl.pallas_call(
         kernel,
         out_shape=out_shape,
@@ -72,12 +72,22 @@
     return exp, sq - TAIL, ex - TAIL, dep - TAIL
 
 
-def pack_kernel(plan, expand, project, squeeze, excite, depth, out):
+def pack_kernel(
+    plan, expand_in, project_in, squeeze_in, excite_in, depth_in, out,
+    expand, project, squeeze, excite, depth, sems,
+):
     exp, sq, ex, dep = plan
+    given = (expand_in, project_in, squeeze_in, excite_in, depth_in)
+    held = (expand, project, squeeze, excite, depth)
+    moves = [pltpu.make_async_copy(a, b, sems.at[k]) for k, (a, b) in enumerate(zip(given, held))]
+    for move in moves:
+        move.start()
     rows, width = project.shape
     c_in = expand.shape[1]
     span = LANES - TAIL
     out[...] = jnp.zeros(out.shape, bf16)
+    for move in moves:
+        move.wait()
     out[0:rows, 0:width] = project[...]
     head = TAIL - exp
     out[0:rows, exp:TAIL] = expand[:, 0:head]
@@ -91,22 +101,26 @@
     tail = place(squeeze[...].astype(bf16), sq)
     tail = tail + place(excite[...].astype(bf16), ex)
     tail = tail + place(top, dep) + place(low, dep + KS * KS)
-    rest = c_in - head
     spot = onehot(iota((c_in, span), 0) == iota((c_in, span), 1) + head)
     tail = tail + dot(expand[...], spot)
-    del rest
     out[0:rows, TAIL:LANES] = tail.astype(bf16)
 
 
 def trunk_kernel(
     plan, n_tokens,
-    ids, cells_ref, film, learner, w,
+    ids, cells_ref, film, learner, packed,
     tokens_out, mixed_out, attend_out, scale_out,
-    e, d, h, wd, exw,
+    w, e, d, h, wd, exw, sems,
 ):
     exp, sq, ex, dep = plan
     width = film.shape[2]
-    hidden = w.shape[0]
+    hidden = packed.shape[0]
+    late, early = (
+        pltpu.make_async_copy(packed.at[:, lanes], w.at[:, lanes], sems.at[k])
+        for k, lanes in enumerate((pl.ds(0, width), pl.ds(width, LANES - width)))
+    )
+    early.start()
+    late.start()
     bands = GRID
     rows = bands * BAND
     n_frames = 3
@@ -129,6 +143,7 @@
         iota((16, LANES - TAIL), 1) == iota((16, LANES - TAIL), 0) + dep + KS * KS
     )
     pick = onehot(pick & (iota((16, LANES - TAIL), 0) < KS * KS))
+    early.wait()
     wd[...] = dot(pick, w[:, TAIL:LANES], NT)
     e[...] = dot(cells_ref[...], w[:, exp:exp + 256], NT)
     place = iota((BAND, 128), 0)
@@ -173,18 +188,21 @@
     )
     mean = dot(onehot(member, f32), exw[...], precision=highest) * (1.0 / (GRID * GRID))
     top, low = halves(mean)
-    both = dot(jnp.concatenate([top, low], axis=0), w[:, TAIL:LANES])
+    stack = jnp.concatenate([top, low], axis=0)
+    both = dot(stack, w[:, TAIL:LANES])
     reduced = both[0:8] + both[8:16]
     turned = pltpu.roll(swish(reduced), ex - sq, 1)
     lane = iota(turned.shape, 1)
     turned = jnp.where((lane >= ex) & (lane < dep), turned, 0.0)
     top, low = halves(turned)
-    both = dot(jnp.concatenate([top, low], axis=0), w[:, TAIL:LANES], NT)
+    stack = jnp.concatenate([top, low], axis=0)
+    both = dot(stack, w[:, TAIL:LANES], NT)
     excite = sigmoid(both[0:8] + both[8:16])
     exw[...] = by_band([excite[f:f + 1] for f in range(n_frames)])
     for r in range(bands):
-        part = slice(r * BAND, (r + 1) * BAND)
-        h[part, :] = (d[part, :] * exw[...]).astype(bf16)
+        band = slice(r * BAND, (r + 1) * BAND)
+        h[band, :] = (d[band, :] * exw[...]).astype(bf16)
+    late.wait()
     block = dot(h[...], w[:, 0:width])
     mixed = (
         block.reshape(bands, BAND, width) * scale_band[None] + shift_band[None]
@@ -197,7 +215,9 @@
     attend = jnp.where(mine, sigmoid(logits), 0.0)
     attend_out[...] = attend
     tokens = dot(attend, mixed, precision=highest) * (1.0 / (GRID * GRID))
-    tokens_out[...] = tokens.astype(bf16)
+    tokens = tokens.astype(bf16)
+    for k in range(tokens_out.shape[0]):
+        tokens_out[k] = tokens
 
 
 def slots_onehot(dest, peers, capacity):
@@ -221,9 +241,14 @@
         out[k] = chosen[k * each:(k + 1) * each].astype(bf16)
 
 
-def backward_kernel(n_tokens, mixed, attend, scale, learner, grads, out):
+def place_of(n_chips):
+    me = lax.axis_index("mp")
+    return me // 2, me % 2, lambda z: lax.rem(z + n_chips, n_chips)
+
+
+def backward_kernel(n_tokens, cells, mixed, attend, scale, learner, grads, same, cross, res):
     n_frames = 3
-    parts, _, share, cells = out.shape
+    chips, share, _ = same.shape
     grad = grads[0].astype(f32)
     for k in range(1, grads.shape[0]):
         grad = grad + grads[k].astype(f32)
@@ -238,11 +263,31 @@
     both = dot(both, onehot(spot, f32), precision=highest)
     factors = jnp.concatenate([grad] + [learner[...]] * n_frames, axis=0)
     for f in range(n_frames):
-        result = dot(
-            factors * scale[f:f + 1, :], both[:, f * 128:(f + 1) * 128], TN, highest
-        )
-        for k in range(parts):
-            out[k, f] = result[k * share:(k + 1) * share, 0:cells].astype(bf16)
+        lanes = slice(f * 128, (f + 1) * 128)
+        res[:, lanes] = dot(factors * scale[f:f + 1, :], both[:, lanes], TN, highest)
+    z, c, wrap = place_of(chips)
+    for k in range(chips):
+        to = 2 * wrap(z + k)
+        for out, owner in ((same, to + c), (cross, to + 1 - c)):
+            out[k] = res[pl.ds(pl.multiple_of(owner * share, 8), share), :].astype(bf16)
+
+
+def pair_kernel(same, cross, *outs):
+    for k, out in enumerate(outs):
+        out[0] = same[k]
+        out[1] = cross[k]
+
+
+def settle_kernel(*refs):
+    *parts, out = refs
+    n_frames = 3
+    cells = out.shape[2]
+    z, c, wrap = place_of(len(parts))
+    for k, part in enumerate(parts):
+        source = 2 * wrap(z - k)
+        for half, owner in ((0, source + c), (1, source + 1 - c)):
+            for f in range(n_frames):
+                out[owner * n_frames + f] = part[half, :, f * 128:f * 128 + cells]
 
 
 def per_device(
@@ -276,13 +321,18 @@
     dest = token_dest.T
     learner = w_learner.T
 
+    raw = (w_expand.T, w_project, w_squeeze.T, w_excite, w_depth)
     mine = call(
         functools.partial(pack_kernel, plan),
         sds((SHARD, LANES), bf16),
-        w_expand.T, w_project, w_squeeze.T, w_excite, w_depth,
-    )
+        *raw,
+        in_specs=[pl.BlockSpec(memory_space=pl.ANY)] * len(raw),
+        scratch=[pltpu.VMEM(a.shape, a.dtype) for a in raw]
+        + [pltpu.SemaphoreType.DMA((len(raw),))],
+        vmem=60,
+    )
+    across = [(m, m ^ 1) for m in range(n_mp)]
     packed = lax.all_gather(mine, "mp", axis=0, tiled=True)
-
     grad_part = dot(policy_cot, w_policy, NT).astype(bf16)
     arrived = lax.all_to_all(
         grad_part.reshape(peers, capacity, width), "seq", split_axis=0, concat_axis=0, tiled=True
@@ -299,45 +349,59 @@
     own = own.transpose(1, 0, 2).reshape(GRID, GRID * n_frames, c_in)
     own = jnp.pad(own, ((0, 0), (0, BAND - GRID * n_frames), (0, 256 - c_in)))
     own = own.reshape(rows, 256)
-    mine, mixed, attend, scale = call(
+    copies, mixed, attend, scale = call(
         functools.partial(trunk_kernel, plan, n_tokens),
         (
-            sds((n_frames * n_tokens, width), bf16),
+            sds((n_mp, n_frames * n_tokens, width), bf16),
             sds((rows, width), f32),
             sds((n_frames * n_tokens, rows), f32),
             sds((8, width), f32),
         ),
         instr_ids, own, film_table, learner, packed,
-        in_specs=[pl.BlockSpec(memory_space=pltpu.SMEM)] + [vmem] * 4,
+        in_specs=[pl.BlockSpec(memory_space=pltpu.SMEM)] + [vmem] * 3 + [pl.BlockSpec(memory_space=pl.ANY)],
         scratch=[
+            pltpu.VMEM((hidden, LANES), bf16),
             pltpu.VMEM((rows, hidden), f32),
             pltpu.VMEM((rows, hidden), f32),
             pltpu.VMEM((rows, hidden), bf16),
             pltpu.VMEM((16, hidden), f32),
             pltpu.VMEM((BAND, hidden), f32),
+            pltpu.SemaphoreType.DMA((2,)),
         ],
-        flops=2e9, moved=3e7,
-    )
-    tokens = lax.all_gather(mine, "mp", axis=0, tiled=True)
+        flops=2e9, moved=3e7, vmem=28,
+    )
+    tokens = lax.all_to_all(copies, "mp", split_axis=0, concat_axis=0, tiled=True)
     outgoing = call(
         functools.partial(scatter_kernel, peers, capacity),
         sds((peers * capacity, width), bf16),
-        tokens, dest,
+        tokens.reshape(count * n_tokens, width), dest,
         flops=3e8, moved=2e6,
     )
+    chips = n_mp // 2
+    half = sds((chips, share, n_frames * 128), bf16)
+    same, cross = call(
+        functools.partial(backward_kernel, n_tokens, cells),
+        (half, half),
+        mixed, attend, scale, learner, grads,
+        scratch=[pltpu.VMEM((width, n_frames * 128), f32)],
+        flops=1e9, moved=2e6,
+    )
+    cross = lax.ppermute(cross, "mp", across)
+    pairs = call(
+        pair_kernel, (sds((2, share, n_frames * 128), bf16),) * chips, same, cross
+    )
+    outgoing, *pairs = lax.optimization_barrier((outgoing, *pairs))
     rows_in = lax.all_to_all(
         outgoing.reshape(peers, capacity, width), "seq", split_axis=0, concat_axis=0, tiled=True
     )
+    parts = [pairs[0]]
+    for k in range(1, chips):
+        parts.append(lax.ppermute(pairs[k], "mp", [(m, (m + 2 * k) % n_mp) for m in range(n_mp)]))
+    feature_grad = call(settle_kernel, sds((count, share, cells), bf16), *parts)
+    w_policy, feature_grad = lax.optimization_barrier((w_policy, feature_grad))
     policy_in = dot(rows_in.reshape(peers * capacity, width), w_policy).astype(bf16)
 
-    parts = call(
-        functools.partial(backward_kernel, n_tokens),
-        sds((n_mp, n_frames, share, cells), bf16),
-        mixed, attend, scale, learner, grads,
-        flops=1e9, moved=2e6,
-    )
-    parts = lax.all_to_all(parts, "mp", split_axis=0, concat_axis=0, tiled=True)
-    feature_grad = parts.reshape(count, share, cells).transpose(0, 2, 1)
+    feature_grad = feature_grad.transpose(0, 2, 1)
     return (policy_in, feature_grad)
 
 

time: 143 us -> 139 us (0.972)
  starting transfers between devices: 28.1 us -> 54.6 us
  blocking collectives: 49.9 us -> 28.4 us
  local copies, waits for them, and re-layouts: 10.3 us -> 3.8 us
  waiting for transfers between devices: 24.4 us -> 18.6 us
  Pallas kernels: 12.1 us -> 14.5 us
    ppermute x0 -> x8, starting transfers between devices: none -> 29 us  [the longest x7 26.7 us: per_device(): lax.ppermute(pairs[k], 'mp', [(m, (m + 2 * k) % n_mp) for m in range(n_mp)])]
    all_gather x1 -> x0, blocking collectives: 21.5 us -> none  [per_device(): tokens = lax.all_gather(mine, 'mp', axis=0, tiled=True)]
    all_to_all x1, waiting for transfers between devices: 18.7 us -> 0.01 us  [per_device(): lax.all_to_all(outgoing.reshape(peers, capacity, width), 'seq', split_axi...]
    unnamed x31 -> x16, local copies, waits for them, and re-layouts: 9.96 us -> 3.49 us
    all_to_all x1, waiting for transfers between devices: 0.01 us -> 5.68 us  [per_device(): lax.all_to_all(copies, 'mp', split_axis=0, concat_axis=0, tiled=True)]
    ppermute x0 -> x8, waiting for transfers between devices: none -> 4.34 us  [the longest x7 3.35 us: per_device(): lax.ppermute(pairs[k], 'mp', [(m, (m + 2 * k) % n_mp) for m in range(n_mp)])]
    all_gather x1, waiting for transfers between devices: 5.61 us -> 8.56 us  [per_device(): packed = lax.all_gather(mine, 'mp', axis=0, tiled=True)]
    pallas_call x5 -> x7, Pallas kernels: 12.1 us -> 14.5 us  [call(): pl.pallas_call(kernel, out_shape=out_shape, in_specs=in_specs or [pl.Bloc...]
  transfers between devices with their start and end apart: 4 -> 12, of which waited for: 2 -> 4; matrix products, arithmetic and copies ran while one was open for 2% -> 2% of each run, Pallas kernels for 6% -> 8%
where the time goes in v2:
time: 139 us; the launch traced here: 138 us
  starting transfers between devices  54.6 us (39%)
  blocking collectives  28.4 us (20%)
  waiting for transfers between devices  18.6 us (13%)
  Pallas kernels  14.5 us (10%)
  between operations  14.3 us (10%)
  matrix products  4.28 us (3%)
  local copies, waits for them, and re-layouts  3.8 us (3%)
    all_to_all x1, blocking collectives, per_device(): lax.all_to_all(grad_part.reshape(peers, capacity, width), 'seq', split_ax...  28.4 us
    ppermute x7, starting transfers between devices, per_device(): lax.ppermute(pairs[k], 'mp', [(m, (m + 2 * k) % n_mp) for m in range(n_mp)])  26.7 us
    pallas_call x7, Pallas kernels, call(): pl.pallas_call(kernel, out_shape=out_shape, in_specs=in_specs or [pl.Bloc...  14.5 us
    all_to_all x1, starting transfers between devices, per_device(): lax.all_to_all(outgoing.reshape(peers, capacity, width), 'seq', split_axi...  10.8 us
    all_to_all x1, starting transfers between devices, per_device(): lax.all_to_all(picked, 'mp', split_axis=0, concat_axis=0, tiled=True)  10.4 us
    all_gather x1, waiting for transfers between devices, per_device(): packed = lax.all_gather(mine, 'mp', axis=0, tiled=True)  8.56 us
    all_to_all x1, waiting for transfers between devices, per_device(): lax.all_to_all(copies, 'mp', split_axis=0, concat_axis=0, tiled=True)  5.68 us
    all_to_all x1, starting transfers between devices, per_device(): lax.all_to_all(copies, 'mp', split_axis=0, concat_axis=0, tiled=True)  4.38 us
  transfers between devices with their start and end apart: 12, of which 4 were waited for; matrix products, arithmetic and copies ran while one was open for 2% of the time, Pallas kernels for 8%

profile of v2, /device:TPU:6, one launch (start us, length us, event | category | flops | bytes accessed | tf_op | source)
XLA Modules:
  0.0 138.5 jit_solution(6086747796034239591)
XLA Ops:
  7.2 2.0 %shard_map.131 = bf16[96,768]{1,0:T(8,128)(2,1)} custom-call(bf16[87,232]{1,0:T(8,128)(2,1)} %bitcast.27, bf16[87,384]{1,0:T(8,128)(2,1)} %project_in.1, f32[58,87]{1,0:T(8,128)} %bitcast.28, f32[58,87]{1,0:T(8,128)} %excite_in.1, f32[9,87]{1,0:T(8,128)} %depth_in.1), custom_call_target="tpu_custom_call" | custom-call | flops 1000000 | bytes 1000000 | tf_op jit(solution)/shard_map/pallas_call | solution.py:54
  9.3 1.8 %convolution_convert_fusion.1 = bf16[768,384]{1,0:T(8,128)(2,1)S(1)} fusion(bf16[768,512]{1,0:T(8,128)(2,1)} %param.23, bf16[384,512]{1,0:T(8,128)(2,1)} %param.22), kind=kOutput, calls=%fused_computation.1 | convolution fusion | flops 302284800 | bytes 1769472 | tf_op jit(solution)/shard_map/dot_general | solution.py:28
  11.2 28.4 %all_to_all.20 = bf16[32,24,384]{2,1,0:T(8,128)(2,1)S(1)} all-to-all(bf16[32,24,384]{2,1,0:T(8,128)(2,1)S(1)} %bitcast.25), channel_id=1, replica_groups=mesh['seq'=32,'mp'=16] {'seq'}, dimensions={0} | all-to-all | bytes 1179648 | tf_op jit(solution)/shard_map/all_to_all | solution.py:337
  39.5 1.4 %shard_map.134 = bf16[16,24,384]{2,1,0:T(8,128)(2,1)} custom-call(bf16[768,384]{1,0:T(8,128)(2,1)S(1)} %bitcast.17, s32[1,384]{1,0:T(1,128)S(1)} %bitcast.22), custom_call_target="tpu_custom_call" | custom-call | flops 300000000 | bytes 2000000 | tf_op jit(solution)/shard_map/pallas_call | solution.py:54
  40.9 10.4 %all-to-all-start.2 = ((bf16[16,24,384]{2,1,0:T(8,128)(2,1)}), bf16[16,24,384]{2,1,0:T(8,128)(2,1)S(1)}, u32[]{:S(2)}, u32[]{:S(2)}) async-start(bf16[16,24,384]{2,1,0:T(8,128)(2,1)} %shard_map.134), calls=%async_computation.2 | async-start | bytes 589824 | tf_op jit(solution)/shard_map/all_to_all | solution.py:346
  51.7 8.6 %all-gather.2.cloned.1.call-done.packed = bf16[1536,768]{1,0:T(8,128)(2,1)} async-done(((bf16[96,768]{1,0:T(8,128)(2,1)}), bf16[1536,768]{1,0:T(8,128)(2,1)}) %all-gather.2.cloned.1.call-update) | async-done | bytes 2359312 | tf_op jit(solution)/shard_map/all_gather | solution.py:335
  60.3 1.7 %copy-done.1 = bf16[1536,768]{1,0:T(8,128)(2,1)S(1)} copy-done((bf16[1536,768]{1,0:T(8,128)(2,1)S(1)}, bf16[1536,768]{1,0:T(8,128)(2,1)}, u32[]{:S(2)}) %copy-start.1) | copy-done | bytes 2359320
  61.9 7.0 %shard_map.132 = (bf16[16,24,384]{2,1,0:T(8,128)(2,1)}, f32[320,384]{1,0:T(8,128)S(1)}, f32[24,320]{1,0:T(8,128)S(1)}, f32[8,384]{1,0:T(8,128)S(1)}) custom-call(s32[48]{0:T(128)S(1)} %copy-done.5, bf16[320,256]{1,0:T(8,128)(2,1)S(1)} %bitcast.19, f32[64,2,384]{2,1,0:T(2,128)S(1)} %copy-done.2, f32[8,384]{1,0:T(8,128)S(1)} %bitcast.20, ...), custom_call_target="tpu_custom_call" | custom-call | flops 2000000000 | bytes 30000000 | tf_op jit(solution)/shard_map/pallas_call | solution.py:54
  69.7 4.4 %all-to-all-start = ((bf16[16,24,384]{2,1,0:T(8,128)(2,1)}), bf16[16,24,384]{2,1,0:T(8,128)(2,1)S(1)}, u32[]{:S(2)}, u32[]{:S(2)}) async-start(bf16[16,24,384]{2,1,0:T(8,128)(2,1)} %get-tuple-element.27), calls=%async_computation | async-start | bytes 589824 | tf_op jit(solution)/shard_map/all_to_all | solution.py:373
  74.1 1.0 copy-done.7
  75.2 1.7 %shard_map.135 = (bf16[8,24,384]{2,1,0:T(8,128)(2,1)S(1)}, bf16[8,24,384]{2,1,0:T(8,128)(2,1)S(1)}) custom-call(f32[320,384]{1,0:T(8,128)S(1)} %copy-done.7, f32[24,320]{1,0:T(8,128)S(1)} %get-tuple-element.29.attend, f32[8,384]{1,0:T(8,128)S(1)} %get-tuple-element.30.scale, f32[8,384]{1,0:T(8,128)S(1)} %bitcast.21, ...), custom_call_target="tpu_custom_call" | custom-call | flops 1000000000 | bytes 2000000 | tf_op jit(solution)/shard_map/pallas_call | solution.py:54
  76.9 2.3 %collective-permute-start = (bf16[8,24,384]{2,1,0:T(8,128)(2,1)S(1)}, bf16[8,24,384]{2,1,0:T(8,128)(2,1)S(1)}, u32[]{:S(2)}, u32[]{:S(2)}) collective-permute-start(bf16[8,24,384]{2,1,0:T(8,128)(2,1)S(1)} %get-tuple-element.32), channel_id=1, source_target_pairs={{0,1},{1,0},{2,3},{3,2},{4,5},{5,4},{6,7},{7,6},{8,9},{9,8},{10,11... | collective-permute-start | bytes 442376 | tf_op jit(solution)/shard_map/ppermute | solution.py:389
  80.2 5.7 %all-to-all-done = bf16[16,24,384]{2,1,0:T(8,128)(2,1)S(1)} async-done(((bf16[16,24,384]{2,1,0:T(8,128)(2,1)}), bf16[16,24,384]{2,1,0:T(8,128)(2,1)S(1)}, u32[]{:S(2)}, u32[]{:S(2)}) %all-to-all-start) | async-done | bytes 294944 | tf_op jit(solution)/shard_map/all_to_all | solution.py:373
  85.9 1.5 %shard_map.133 = bf16[768,384]{1,0:T(8,128)(2,1)} custom-call(bf16[384,384]{1,0:T(8,128)(2,1)S(1)} %bitcast.18, s32[1,384]{1,0:T(1,128)S(1)} %bitcast.23), custom_call_target="tpu_custom_call" | custom-call | flops 300000000 | bytes 2000000 | tf_op jit(solution)/shard_map/pallas_call | solution.py:54
  87.4 10.8 %all-to-all-start.3 = ((bf16[32,24,384]{2,1,0:T(8,128)(2,1)}), bf16[32,24,384]{2,1,0:T(8,128)(2,1)S(1)}, u32[]{:S(2)}, u32[]{:S(2)}) async-start(bf16[32,24,384]{2,1,0:T(8,128)(2,1)} %bitcast.9), calls=%async_computation.3 | async-start | bytes 1179648 | tf_op jit(solution)/shard_map/all_to_all | solution.py:394
  98.2 2.2 %collective-permute-start.1 = (bf16[2,24,384]{2,1,0:T(8,128)(2,1)S(1)}, bf16[2,24,384]{2,1,0:T(8,128)(2,1)S(1)}, u32[]{:S(2)}, u32[]{:S(2)}) collective-permute-start(bf16[2,24,384]{2,1,0:T(8,128)(2,1)S(1)} %get-tuple-element.43), channel_id=1, source_target_pairs={{0,2},{1,3},{2,4},{3,5},{4,6},{5,7},{6,8},{7,9},{8,10},{9,11},{10,... | collective-permute-start | bytes 110600 | tf_op jit(solution)/shard_map/ppermute | solution.py:399
  100.5 4.2 %collective-permute-start.2 = (bf16[2,24,384]{2,1,0:T(8,128)(2,1)S(1)}, bf16[2,24,384]{2,1,0:T(8,128)(2,1)S(1)}, u32[]{:S(2)}, u32[]{:S(2)}) collective-permute-start(bf16[2,24,384]{2,1,0:T(8,128)(2,1)S(1)} %get-tuple-element.44), channel_id=1, source_target_pairs={{0,4},{1,5},{2,6},{3,7},{4,8},{5,9},{6,10},{7,11},{8,12},{9,13},{1... | collective-permute-start | bytes 110600 | tf_op jit(solution)/shard_map/ppermute | solution.py:399
  104.7 3.8 %collective-permute-start.3 = (bf16[2,24,384]{2,1,0:T(8,128)(2,1)S(1)}, bf16[2,24,384]{2,1,0:T(8,128)(2,1)S(1)}, u32[]{:S(2)}, u32[]{:S(2)}) collective-permute-start(bf16[2,24,384]{2,1,0:T(8,128)(2,1)S(1)} %get-tuple-element.45), channel_id=1, source_target_pairs={{0,6},{1,7},{2,8},{3,9},{4,10},{5,11},{6,12},{7,13},{8,14},{9,15},... | collective-permute-start | bytes 110600 | tf_op jit(solution)/shard_map/ppermute | solution.py:399
  108.5 5.4 %collective-permute-start.4 = (bf16[2,24,384]{2,1,0:T(8,128)(2,1)S(1)}, bf16[2,24,384]{2,1,0:T(8,128)(2,1)S(1)}, u32[]{:S(2)}, u32[]{:S(2)}) collective-permute-start(bf16[2,24,384]{2,1,0:T(8,128)(2,1)S(1)} %get-tuple-element.46), channel_id=1, source_target_pairs={{0,8},{1,9},{2,10},{3,11},{4,12},{5,13},{6,14},{7,15},{8,0},{9,1},... | collective-permute-start | bytes 110600 | tf_op jit(solution)/shard_map/ppermute | solution.py:399
  113.8 2.9 %collective-permute-start.5 = (bf16[2,24,384]{2,1,0:T(8,128)(2,1)S(1)}, bf16[2,24,384]{2,1,0:T(8,128)(2,1)S(1)}, u32[]{:S(2)}, u32[]{:S(2)}) collective-permute-start(bf16[2,24,384]{2,1,0:T(8,128)(2,1)S(1)} %get-tuple-element.47), channel_id=1, source_target_pairs={{0,10},{1,11},{2,12},{3,13},{4,14},{5,15},{6,0},{7,1},{8,2},{9,3},... | collective-permute-start | bytes 110600 | tf_op jit(solution)/shard_map/ppermute | solution.py:399
  116.8 5.7 %collective-permute-start.6 = (bf16[2,24,384]{2,1,0:T(8,128)(2,1)S(1)}, bf16[2,24,384]{2,1,0:T(8,128)(2,1)S(1)}, u32[]{:S(2)}, u32[]{:S(2)}) collective-permute-start(bf16[2,24,384]{2,1,0:T(8,128)(2,1)S(1)} %get-tuple-element.48), channel_id=1, source_target_pairs={{0,12},{1,13},{2,14},{3,15},{4,0},{5,1},{6,2},{7,3},{8,4},{9,5},{1... | collective-permute-start | bytes 110600 | tf_op jit(solution)/shard_map/ppermute | solution.py:399
  122.5 2.5 %collective-permute-start.7 = (bf16[2,24,384]{2,1,0:T(8,128)(2,1)S(1)}, bf16[2,24,384]{2,1,0:T(8,128)(2,1)S(1)}, u32[]{:S(2)}, u32[]{:S(2)}) collective-permute-start(bf16[2,24,384]{2,1,0:T(8,128)(2,1)S(1)} %get-tuple-element.49), channel_id=1, source_target_pairs={{0,14},{1,15},{2,0},{3,1},{4,2},{5,3},{6,4},{7,5},{8,6},{9,7},{10,... | collective-permute-start | bytes 110600 | tf_op jit(solution)/shard_map/ppermute | solution.py:399
  125.1 3.3 %collective-permute-done.7.refs_7_ = bf16[2,24,384]{2,1,0:T(8,128)(2,1)S(1)} collective-permute-done((bf16[2,24,384]{2,1,0:T(8,128)(2,1)S(1)}, bf16[2,24,384]{2,1,0:T(8,128)(2,1)S(1)}, u32[]{:S(2)}, u32[]{:S(2)}) %collective-permute-start.7) | collective-permute-done | bytes 36896 | tf_op jit(solution)/shard_map/ppermute | solution.py:399
  129.2 2.5 %convolution_convert_fusion = bf16[768,512]{1,0:T(8,128)(2,1)} fusion(bf16[768,384]{1,0:T(8,128)(2,1)S(1)} %bitcast.24, bf16[384,512]{1,0:T(8,128)(2,1)} %param.22), kind=kOutput, calls=%fused_computation | convolution fusion | flops 302383104 | bytes 1769472 | tf_op jit(solution)/shard_map/dot_general | solution.py:28
  (30 shorter events, 3.0 us)
Async XLA Ops:
  7.2 44.2 %copy-start = (bf16[48,100,232]{2,0,1:T(8,128)(2,1)S(1)}, bf16[48,100,232]{2,0,1:T(8,128)(2,1)}, u32[]{:S(2)}) copy-start(bf16[48,100,232]{2,0,1:T(8,128)(2,1)} %param.12) | copy-start | bytes 6681604
  7.2 32.3 %copy-start.4 = (s32[384,1]{0,1:T(1,128)S(1)}, s32[384,1]{0,1:T(1,128)}, u32[]{:S(2)}) copy-start(s32[384,1]{0,1:T(1,128)} %param.21) | copy-start | bytes 4612
  7.2 53.1 %all-gather.2.cloned.1.call-start = ((), (), s32[]{:S(2)}) async-start(), calls=%async_computation.4 | async-start | bytes 2506752 | tf_op jit(solution)/shard_map/all_gather | solution.py:335
  11.1 49.1 %copy-start.2 = (f32[64,2,384]{2,1,0:T(2,128)S(1)}, f32[64,2,384]{2,1,0:T(2,128)}, u32[]{:S(2)}) copy-start(f32[64,2,384]{2,1,0:T(2,128)} %film.1) | copy-start | bytes 589828
  11.1 49.1 %copy-start.3 = (f32[384,8]{0,1:T(8,128)S(1)}, f32[384,8]{0,1:T(8,128)}, u32[]{:S(2)}) copy-start(f32[384,8]{0,1:T(8,128)} %param.20) | copy-start | bytes 36868
  11.1 49.1 %copy-start.5 = (s32[48]{0:T(128)S(1)}, s32[48]{0:T(128)}, u32[]{:S(2)}) copy-start(s32[48]{0:T(128)} %ids.1) | copy-start | bytes 580
  40.9 28.8 %all-to-all-start.2 = ((bf16[16,24,384]{2,1,0:T(8,128)(2,1)}), bf16[16,24,384]{2,1,0:T(8,128)(2,1)S(1)}, u32[]{:S(2)}, u32[]{:S(2)}) async-start(bf16[16,24,384]{2,1,0:T(8,128)(2,1)} %shard_map.134), calls=%async_computation.2 | async-start | bytes 589824 | tf_op jit(solution)/shard_map/all_to_all | solution.py:346
  60.3 1.7 %copy-start.1 = (bf16[1536,768]{1,0:T(8,128)(2,1)S(1)}, bf16[1536,768]{1,0:T(8,128)(2,1)}, u32[]{:S(2)}) copy-start(bf16[1536,768]{1,0:T(8,128)(2,1)} %all-gather.2.cloned.1.call-done.packed) | copy-start | bytes 7077892
  69.0 0.8 copy-start.6
  69.7 16.2 %all-to-all-start = ((bf16[16,24,384]{2,1,0:T(8,128)(2,1)}), bf16[16,24,384]{2,1,0:T(8,128)(2,1)S(1)}, u32[]{:S(2)}, u32[]{:S(2)}) async-start(bf16[16,24,384]{2,1,0:T(8,128)(2,1)} %get-tuple-element.27), calls=%async_computation | async-start | bytes 589824 | tf_op jit(solution)/shard_map/all_to_all | solution.py:373
  74.1 1.0 copy-start.7
  76.9 3.3 %collective-permute-start = (bf16[8,24,384]{2,1,0:T(8,128)(2,1)S(1)}, bf16[8,24,384]{2,1,0:T(8,128)(2,1)S(1)}, u32[]{:S(2)}, u32[]{:S(2)}) collective-permute-start(bf16[8,24,384]{2,1,0:T(8,128)(2,1)S(1)} %get-tuple-element.32), channel_id=1, source_target_pairs={{0,1},{1,0},{2,3},{3,2},{4,5},{5,4},{6,7},{7,6},{8,9},{9,8},{10,11... | collective-permute-start | bytes 442376 | tf_op jit(solution)/shard_map/ppermute | solution.py:389
  87.4 41.7 %all-to-all-start.3 = ((bf16[32,24,384]{2,1,0:T(8,128)(2,1)}), bf16[32,24,384]{2,1,0:T(8,128)(2,1)S(1)}, u32[]{:S(2)}, u32[]{:S(2)}) async-start(bf16[32,24,384]{2,1,0:T(8,128)(2,1)} %bitcast.9), calls=%async_computation.3 | async-start | bytes 1179648 | tf_op jit(solution)/shard_map/all_to_all | solution.py:394
  98.2 18.5 %collective-permute-start.1 = (bf16[2,24,384]{2,1,0:T(8,128)(2,1)S(1)}, bf16[2,24,384]{2,1,0:T(8,128)(2,1)S(1)}, u32[]{:S(2)}, u32[]{:S(2)}) collective-permute-start(bf16[2,24,384]{2,1,0:T(8,128)(2,1)S(1)} %get-tuple-element.43), channel_id=1, source_target_pairs={{0,2},{1,3},{2,4},{3,5},{4,6},{5,7},{6,8},{7,9},{8,10},{9,11},{10,... | collective-permute-start | bytes 110600 | tf_op jit(solution)/shard_map/ppermute | solution.py:399
  100.5 22.1 %collective-permute-start.2 = (bf16[2,24,384]{2,1,0:T(8,128)(2,1)S(1)}, bf16[2,24,384]{2,1,0:T(8,128)(2,1)S(1)}, u32[]{:S(2)}, u32[]{:S(2)}) collective-permute-start(bf16[2,24,384]{2,1,0:T(8,128)(2,1)S(1)} %get-tuple-element.44), channel_id=1, source_target_pairs={{0,4},{1,5},{2,6},{3,7},{4,8},{5,9},{6,10},{7,11},{8,12},{9,13},{1... | collective-permute-start | bytes 110600 | tf_op jit(solution)/shard_map/ppermute | solution.py:399
  104.7 20.3 %collective-permute-start.3 = (bf16[2,24,384]{2,1,0:T(8,128)(2,1)S(1)}, bf16[2,24,384]{2,1,0:T(8,128)(2,1)S(1)}, u32[]{:S(2)}, u32[]{:S(2)}) collective-permute-start(bf16[2,24,384]{2,1,0:T(8,128)(2,1)S(1)} %get-tuple-element.45), channel_id=1, source_target_pairs={{0,6},{1,7},{2,8},{3,9},{4,10},{5,11},{6,12},{7,13},{8,14},{9,15},... | collective-permute-start | bytes 110600 | tf_op jit(solution)/shard_map/ppermute | solution.py:399
  108.5 16.6 %collective-permute-start.4 = (bf16[2,24,384]{2,1,0:T(8,128)(2,1)S(1)}, bf16[2,24,384]{2,1,0:T(8,128)(2,1)S(1)}, u32[]{:S(2)}, u32[]{:S(2)}) collective-permute-start(bf16[2,24,384]{2,1,0:T(8,128)(2,1)S(1)} %get-tuple-element.46), channel_id=1, source_target_pairs={{0,8},{1,9},{2,10},{3,11},{4,12},{5,13},{6,14},{7,15},{8,0},{9,1},... | collective-permute-start | bytes 110600 | tf_op jit(solution)/shard_map/ppermute | solution.py:399
  113.8 11.2 %collective-permute-start.5 = (bf16[2,24,384]{2,1,0:T(8,128)(2,1)S(1)}, bf16[2,24,384]{2,1,0:T(8,128)(2,1)S(1)}, u32[]{:S(2)}, u32[]{:S(2)}) collective-permute-start(bf16[2,24,384]{2,1,0:T(8,128)(2,1)S(1)} %get-tuple-element.47), channel_id=1, source_target_pairs={{0,10},{1,11},{2,12},{3,13},{4,14},{5,15},{6,0},{7,1},{8,2},{9,3},... | collective-permute-start | bytes 110600 | tf_op jit(solution)/shard_map/ppermute | solution.py:399
  116.8 8.2 %collective-permute-start.6 = (bf16[2,24,384]{2,1,0:T(8,128)(2,1)S(1)}, bf16[2,24,384]{2,1,0:T(8,128)(2,1)S(1)}, u32[]{:S(2)}, u32[]{:S(2)}) collective-permute-start(bf16[2,24,384]{2,1,0:T(8,128)(2,1)S(1)} %get-tuple-element.48), channel_id=1, source_target_pairs={{0,12},{1,13},{2,14},{3,15},{4,0},{5,1},{6,2},{7,3},{8,4},{9,5},{1... | collective-permute-start | bytes 110600 | tf_op jit(solution)/shard_map/ppermute | solution.py:399
  122.5 5.9 %collective-permute-start.7 = (bf16[2,24,384]{2,1,0:T(8,128)(2,1)S(1)}, bf16[2,24,384]{2,1,0:T(8,128)(2,1)S(1)}, u32[]{:S(2)}, u32[]{:S(2)}) collective-permute-start(bf16[2,24,384]{2,1,0:T(8,128)(2,1)S(1)} %get-tuple-element.49), channel_id=1, source_target_pairs={{0,14},{1,15},{2,0},{3,1},{4,2},{5,3},{6,4},{7,5},{8,6},{9,7},{10,... | collective-permute-start | bytes 110600 | tf_op jit(solution)/shard_map/ppermute | solution.py:399
Sparse Core Ops, SparseCore 0:
  10.7 49.4 all-gather.1

commit v3 on v2

--- a/solution.py
+++ b/solution.py
@@ -10,7 +10,7 @@
 KS = 3
 GRID = 10
 BAND = 32
-SHARD = 96
+SHARD = 88
 LANES = 768
 TAIL = 512
 MIB = 1024 * 1024
@@ -241,14 +241,9 @@
         out[k] = chosen[k * each:(k + 1) * each].astype(bf16)
 
 
-def place_of(n_chips):
-    me = lax.axis_index("mp")
-    return me // 2, me % 2, lambda z: lax.rem(z + n_chips, n_chips)
-
-
-def backward_kernel(n_tokens, cells, mixed, attend, scale, learner, grads, same, cross, res):
+def backward_kernel(n_tokens, cells, mixed, attend, scale, learner, grads, kept, sent, res):
     n_frames = 3
-    chips, share, _ = same.shape
+    share = kept.shape[1]
     grad = grads[0].astype(f32)
     for k in range(1, grads.shape[0]):
         grad = grad + grads[k].astype(f32)
@@ -265,29 +260,29 @@
     for f in range(n_frames):
         lanes = slice(f * 128, (f + 1) * 128)
         res[:, lanes] = dot(factors * scale[f:f + 1, :], both[:, lanes], TN, highest)
-    z, c, wrap = place_of(chips)
-    for k in range(chips):
-        to = 2 * wrap(z + k)
-        for out, owner in ((same, to + c), (cross, to + 1 - c)):
-            out[k] = res[pl.ds(pl.multiple_of(owner * share, 8), share), :].astype(bf16)
-
-
-def pair_kernel(same, cross, *outs):
-    for k, out in enumerate(outs):
-        out[0] = same[k]
-        out[1] = cross[k]
-
-
-def settle_kernel(*refs):
+    me = lax.axis_index("mp")
+    for k in range(kept.shape[0]):
+        apart = 2 * sum(((k >> bit) & 1) << (2 - bit) for bit in range(3))
+        for out, far in ((kept, apart), (sent, apart + 1)):
+            first = pl.multiple_of(lax.bitwise_xor(me, far) * share, 8)
+            out[k] = res[pl.ds(first, share), :].astype(bf16)
+
+
+def join_kernel(wanted, *refs):
+    *parts, out = refs
+    for k, (part, block) in enumerate(wanted):
+        out[k] = parts[part][block]
+
+
+def settle_kernel(wanted, *refs):
     *parts, out = refs
     n_frames = 3
     cells = out.shape[2]
-    z, c, wrap = place_of(len(parts))
-    for k, part in enumerate(parts):
-        source = 2 * wrap(z - k)
-        for half, owner in ((0, source + c), (1, source + 1 - c)):
-            for f in range(n_frames):
-                out[owner * n_frames + f] = part[half, :, f * 128:f * 128 + cells]
+    me = lax.axis_index("mp")
+    for k, (part, block) in enumerate(wanted):
+        source = lax.bitwise_xor(me, k) * n_frames
+        for f in range(n_frames):
+            out[source + f] = parts[part][block, :, f * 128:f * 128 + cells]
 
 
 def per_device(
@@ -368,7 +363,7 @@
             pltpu.VMEM((BAND, hidden), f32),
             pltpu.SemaphoreType.DMA((2,)),
         ],
-        flops=2e9, moved=3e7, vmem=28,
+        flops=2e9, moved=3e7, vmem=58,
     )
     tokens = lax.all_to_all(copies, "mp", split_axis=0, concat_axis=0, tiled=True)
     outgoing = call(
@@ -377,27 +372,34 @@
         tokens.reshape(count * n_tokens, width), dest,
         flops=3e8, moved=2e6,
     )
-    chips = n_mp // 2
-    half = sds((chips, share, n_frames * 128), bf16)
-    same, cross = call(
+    blocks = sds((n_mp // 2, share, n_frames * 128), bf16)
+    kept, sent = call(
         functools.partial(backward_kernel, n_tokens, cells),
-        (half, half),
+        (blocks, blocks),
         mixed, attend, scale, learner, grads,
         scratch=[pltpu.VMEM((width, n_frames * 128), f32)],
         flops=1e9, moved=2e6,
     )
-    cross = lax.ppermute(cross, "mp", across)
-    pairs = call(
-        pair_kernel, (sds((2, share, n_frames * 128), bf16),) * chips, same, cross
-    )
-    outgoing, *pairs = lax.optimization_barrier((outgoing, *pairs))
+
+    def swap(value, bit):
+        return lax.ppermute(value, "mp", [(m, m ^ bit) for m in range(n_mp)])
+
+    parts = [kept, swap(sent, 1)]
+    groups = [(0, 0), (1, 0)]
+    for step, bit in enumerate((2, 4, 8)):
+        held = 4 >> step
+        if bit == 4:
+            outgoing, *parts = lax.optimization_barrier((outgoing, *parts))
+        wanted = [(p, first + held + k) for p, first in groups for k in range(held)]
+        sent = call(functools.partial(join_kernel, wanted), blocks, *parts)
+        groups = groups + [(len(parts), held * k) for k in range(len(groups))]
+        parts = parts + [swap(sent, bit)]
     rows_in = lax.all_to_all(
         outgoing.reshape(peers, capacity, width), "seq", split_axis=0, concat_axis=0, tiled=True
     )
-    parts = [pairs[0]]
-    for k in range(1, chips):
-        parts.append(lax.ppermute(pairs[k], "mp", [(m, (m + 2 * k) % n_mp) for m in range(n_mp)]))
-    feature_grad = call(settle_kernel, sds((count, share, cells), bf16), *parts)
+    feature_grad = call(
+        functools.partial(settle_kernel, groups), sds((count, share, cells), bf16), *parts
+    )
     w_policy, feature_grad = lax.optimization_barrier((w_policy, feature_grad))
     policy_in = dot(rows_in.reshape(peers * capacity, width), w_policy).astype(bf16)
 

time: 139 us -> 135 us (0.971)
  starting transfers between devices: 54.6 us -> 43.4 us
  waiting for transfers between devices: 18.6 us -> 24.4 us
    ppermute x8 -> x4, waiting for transfers between devices: 4.34 us -> 16.1 us  [swap(): return lax.ppermute(value, 'mp', [(m, m ^ bit) for m in range(n_mp)])]
    ppermute x8 -> x4, starting transfers between devices: 29 us -> 17.8 us  [swap(): return lax.ppermute(value, 'mp', [(m, m ^ bit) for m in range(n_mp)])]
    all_to_all x1, waiting for transfers between devices: 5.68 us -> 0.41 us  [per_device(): lax.all_to_all(copies, 'mp', split_axis=0, concat_axis=0, tiled=True)]
    pallas_call x7 -> x9, Pallas kernels: 14.5 us -> 15.7 us  [call(): pl.pallas_call(kernel, out_shape=out_shape, in_specs=in_specs or [pl.Bloc...]
    unnamed x16 -> x12, local copies, waits for them, and re-layouts: 3.49 us -> 2.52 us
  transfers between devices with their start and end apart: 12 -> 8, of which waited for: 4 -> 6; matrix products, arithmetic and copies ran while one was open for 2% -> 2% of each run, Pallas kernels for 8% -> 10%
where the time goes in v3:
time: 135 us; the launch traced here: 134 us
  starting transfers between devices  43.4 us (32%)
  blocking collectives  28.2 us (21%)
  waiting for transfers between devices  24.4 us (18%)
  Pallas kernels  15.7 us (12%)
  between operations  14.2 us (11%)
  matrix products  4.28 us (3%)
  local copies, waits for them, and re-layouts  3.48 us (3%)
    all_to_all x1, blocking collectives, per_device(): lax.all_to_all(grad_part.reshape(peers, capacity, width), 'seq', split_ax...  28.2 us
    ppermute x4, starting transfers between devices, swap(): return lax.ppermute(value, 'mp', [(m, m ^ bit) for m in range(n_mp)])  17.8 us
    ppermute x4, waiting for transfers between devices, swap(): return lax.ppermute(value, 'mp', [(m, m ^ bit) for m in range(n_mp)])  16.1 us
    pallas_call x9, Pallas kernels, call(): pl.pallas_call(kernel, out_shape=out_shape, in_specs=in_specs or [pl.Bloc...  15.7 us
    all_to_all x1, starting transfers between devices, per_device(): lax.all_to_all(outgoing.reshape(peers, capacity, width), 'seq', split_axi...  10.9 us
    all_to_all x1, starting transfers between devices, per_device(): lax.all_to_all(picked, 'mp', split_axis=0, concat_axis=0, tiled=True)  10.4 us
    all_gather x1, waiting for transfers between devices, per_device(): packed = lax.all_gather(mine, 'mp', axis=0, tiled=True)  7.91 us
    dot_general x2, matrix products, dot(): lax.dot_general(a, b, dims, precision=precision, preferred_element_type=f32)  4.28 us
  transfers between devices with their start and end apart: 8, of which 6 were waited for; matrix products, arithmetic and copies ran while one was open for 2% of the time, Pallas kernels for 10%

profile of v3, /device:TPU:6, one launch (start us, length us, event | category | flops | bytes accessed | tf_op | source)
XLA Modules:
  0.0 133.7 jit_solution(9788186531479193437)
XLA Ops:
  7.2 2.0 %shard_map.131 = bf16[88,768]{1,0:T(8,128)(2,1)} custom-call(bf16[87,232]{1,0:T(8,128)(2,1)} %bitcast.27, bf16[87,384]{1,0:T(8,128)(2,1)} %project_in.1, f32[58,87]{1,0:T(8,128)} %bitcast.28, f32[58,87]{1,0:T(8,128)} %excite_in.1, f32[9,87]{1,0:T(8,128)} %depth_in.1), custom_call_target="tpu_custom_call" | custom-call | flops 1000000 | bytes 1000000 | tf_op jit(solution)/shard_map/pallas_call | solution.py:54
  9.3 1.8 %convolution_convert_fusion.1 = bf16[768,384]{1,0:T(8,128)(2,1)S(1)} fusion(bf16[768,512]{1,0:T(8,128)(2,1)} %param.23, bf16[384,512]{1,0:T(8,128)(2,1)} %param.22), kind=kOutput, calls=%fused_computation.1 | convolution fusion | flops 302284800 | bytes 1769472 | tf_op jit(solution)/shard_map/dot_general | solution.py:28
  11.1 28.2 %all_to_all.20 = bf16[32,24,384]{2,1,0:T(8,128)(2,1)S(1)} all-to-all(bf16[32,24,384]{2,1,0:T(8,128)(2,1)S(1)} %bitcast.24), channel_id=1, replica_groups=mesh['seq'=32,'mp'=16] {'seq'}, dimensions={0} | all-to-all | bytes 1179648 | tf_op jit(solution)/shard_map/all_to_all | solution.py:332
  39.3 1.4 %shard_map.134 = bf16[16,24,384]{2,1,0:T(8,128)(2,1)} custom-call(bf16[768,384]{1,0:T(8,128)(2,1)S(1)} %bitcast.17, s32[1,384]{1,0:T(1,128)S(1)} %bitcast.21), custom_call_target="tpu_custom_call" | custom-call | flops 300000000 | bytes 2000000 | tf_op jit(solution)/shard_map/pallas_call | solution.py:54
  40.7 10.4 %all-to-all-start.2 = ((bf16[16,24,384]{2,1,0:T(8,128)(2,1)}), bf16[16,24,384]{2,1,0:T(8,128)(2,1)S(1)}, u32[]{:S(2)}, u32[]{:S(2)}) async-start(bf16[16,24,384]{2,1,0:T(8,128)(2,1)} %shard_map.134), calls=%async_computation.2 | async-start | bytes 589824 | tf_op jit(solution)/shard_map/all_to_all | solution.py:341
  52.2 7.9 %all-gather.2.cloned.1.call-done.packed = bf16[1408,768]{1,0:T(8,128)(2,1)} async-done(((bf16[88,768]{1,0:T(8,128)(2,1)}), bf16[1408,768]{1,0:T(8,128)(2,1)}) %all-gather.2.cloned.1.call-update) | async-done | bytes 2162704 | tf_op jit(solution)/shard_map/all_gather | solution.py:330
  60.1 8.2 %shard_map.132 = (bf16[16,24,384]{2,1,0:T(8,128)(2,1)}, f32[320,384]{1,0:T(8,128)}, f32[24,320]{1,0:T(8,128)}, f32[8,384]{1,0:T(8,128)}) custom-call(s32[48]{0:T(128)} %ids.1, bf16[320,256]{1,0:T(8,128)(2,1)} %bitcast.26, f32[64,2,384]{2,1,0:T(2,128)} %film.1, f32[8,384]{1,0:T(8,128)} %bitcast.19, bf16[1408,768]{1,0:T(8,128)(2,1)} %all-gather.2.cloned.1.call-done.packed), custom_call_target="tpu_custom_call" | custom-call | flops 2000000000 | bytes 30000000 | tf_op jit(solution)/shard_map/pallas_call | solution.py:54
  68.3 4.2 %all-to-all-start = ((bf16[16,24,384]{2,1,0:T(8,128)(2,1)}), bf16[16,24,384]{2,1,0:T(8,128)(2,1)S(1)}, u32[]{:S(2)}, u32[]{:S(2)}) async-start(bf16[16,24,384]{2,1,0:T(8,128)(2,1)} %get-tuple-element.14), calls=%async_computation | async-start | bytes 589824 | tf_op jit(solution)/shard_map/all_to_all | solution.py:368
  72.6 1.0 copy-done.3
  73.6 0.8 copy-done.4
  74.4 0.7 copy-done.5
  75.1 1.7 %shard_map.135 = (bf16[8,24,384]{2,1,0:T(8,128)(2,1)S(1)}, bf16[8,24,384]{2,1,0:T(8,128)(2,1)S(1)}) custom-call(f32[320,384]{1,0:T(8,128)S(1)} %copy-done.3, f32[24,320]{1,0:T(8,128)S(1)} %copy-done.4, f32[8,384]{1,0:T(8,128)S(1)} %copy-done.5, f32[8,384]{1,0:T(8,128)S(1)} %bitcast.20, bf16[16,24,384]{2,1,0:T(8,128)(2,1)S(1)} %all-to-all-done.2.grads), custom_call_target="tpu_custom_call" | custom-call | flops 1000000000 | bytes 2000000 | tf_op jit(solution)/shard_map/pallas_call | solution.py:54
  76.8 2.3 %collective-permute-start = (bf16[8,24,384]{2,1,0:T(8,128)(2,1)S(1)}, bf16[8,24,384]{2,1,0:T(8,128)(2,1)S(1)}, u32[]{:S(2)}, u32[]{:S(2)}) collective-permute-start(bf16[8,24,384]{2,1,0:T(8,128)(2,1)S(1)} %get-tuple-element.19), channel_id=1, source_target_pairs={{0,1},{1,0},{2,3},{3,2},{4,5},{5,4},{6,7},{7,6},{8,9},{9,8},{10,11... | collective-permute-start | bytes 442376 | tf_op jit(solution)/shard_map/ppermute | solution.py:385
  79.1 1.0 collective-permute-done.refs_1_
  80.1 3.8 %collective-permute-start.1 = (bf16[8,24,384]{2,1,0:T(8,128)(2,1)S(1)}, bf16[8,24,384]{2,1,0:T(8,128)(2,1)S(1)}, u32[]{:S(2)}, u32[]{:S(2)}) collective-permute-start(bf16[8,24,384]{2,1,0:T(8,128)(2,1)S(1)} %shard_map.136), channel_id=1, source_target_pairs={{0,2},{1,3},{2,0},{3,1},{4,6},{5,7},{6,4},{7,5},{8,10},{9,11},{10,... | collective-permute-start | bytes 442376 | tf_op jit(solution)/shard_map/ppermute | solution.py:385
  84.3 1.5 %shard_map.133 = bf16[768,384]{1,0:T(8,128)(2,1)} custom-call(bf16[384,384]{1,0:T(8,128)(2,1)S(1)} %bitcast.18, s32[1,384]{1,0:T(1,128)S(1)} %bitcast.22), custom_call_target="tpu_custom_call" | custom-call | flops 300000000 | bytes 2000000 | tf_op jit(solution)/shard_map/pallas_call | solution.py:54
  85.9 2.3 %collective-permute-done.1.refs_2_ = bf16[8,24,384]{2,1,0:T(8,128)(2,1)S(1)} collective-permute-done((bf16[8,24,384]{2,1,0:T(8,128)(2,1)S(1)}, bf16[8,24,384]{2,1,0:T(8,128)(2,1)S(1)}, u32[]{:S(2)}, u32[]{:S(2)}) %collective-permute-start.1) | collective-permute-done | bytes 147488 | tf_op jit(solution)/shard_map/ppermute | solution.py:385
  88.1 10.9 %all-to-all-start.3 = ((bf16[32,24,384]{2,1,0:T(8,128)(2,1)}), bf16[32,24,384]{2,1,0:T(8,128)(2,1)S(1)}, u32[]{:S(2)}, u32[]{:S(2)}) async-start(bf16[32,24,384]{2,1,0:T(8,128)(2,1)} %bitcast.9), calls=%async_computation.3 | async-start | bytes 1179648 | tf_op jit(solution)/shard_map/all_to_all | solution.py:397
  99.0 4.5 %collective-permute-start.2 = (bf16[8,24,384]{2,1,0:T(8,128)(2,1)S(1)}, bf16[8,24,384]{2,1,0:T(8,128)(2,1)S(1)}, u32[]{:S(2)}, u32[]{:S(2)}) collective-permute-start(bf16[8,24,384]{2,1,0:T(8,128)(2,1)S(1)} %shard_map.137), channel_id=1, source_target_pairs={{0,4},{1,5},{2,6},{3,7},{4,0},{5,1},{6,2},{7,3},{8,12},{9,13},{10,... | collective-permute-start | bytes 442376 | tf_op jit(solution)/shard_map/ppermute | solution.py:385
  103.5 6.2 %collective-permute-done.2.refs_3_ = bf16[8,24,384]{2,1,0:T(8,128)(2,1)S(1)} collective-permute-done((bf16[8,24,384]{2,1,0:T(8,128)(2,1)S(1)}, bf16[8,24,384]{2,1,0:T(8,128)(2,1)S(1)}, u32[]{:S(2)}, u32[]{:S(2)}) %collective-permute-start.2) | collective-permute-done | bytes 147488 | tf_op jit(solution)/shard_map/ppermute | solution.py:385
  109.7 7.3 %collective-permute-start.3 = (bf16[8,24,384]{2,1,0:T(8,128)(2,1)S(1)}, bf16[8,24,384]{2,1,0:T(8,128)(2,1)S(1)}, u32[]{:S(2)}, u32[]{:S(2)}) collective-permute-start(bf16[8,24,384]{2,1,0:T(8,128)(2,1)S(1)} %shard_map.138), channel_id=1, source_target_pairs={{0,8},{1,9},{2,10},{3,11},{4,12},{5,13},{6,14},{7,15},{8,0},{9,1},... | collective-permute-start | bytes 442376 | tf_op jit(solution)/shard_map/ppermute | solution.py:385
  117.0 6.6 %collective-permute-done.3.refs_4_ = bf16[8,24,384]{2,1,0:T(8,128)(2,1)S(1)} collective-permute-done((bf16[8,24,384]{2,1,0:T(8,128)(2,1)S(1)}, bf16[8,24,384]{2,1,0:T(8,128)(2,1)S(1)}, u32[]{:S(2)}, u32[]{:S(2)}) %collective-permute-start.3) | collective-permute-done | bytes 147488 | tf_op jit(solution)/shard_map/ppermute | solution.py:385
  123.6 0.8 shard_map.139
  124.4 2.5 %convolution_convert_fusion = bf16[768,512]{1,0:T(8,128)(2,1)} fusion(bf16[768,384]{1,0:T(8,128)(2,1)S(1)} %bitcast.23, bf16[384,512]{1,0:T(8,128)(2,1)} %param.22), kind=kOutput, calls=%fused_computation | convolution fusion | flops 302383104 | bytes 1769472 | tf_op jit(solution)/shard_map/dot_general | solution.py:28
  (20 shorter events, 1.5 us)
Async XLA Ops:
  7.2 44.0 %copy-start = (bf16[48,100,232]{2,0,1:T(8,128)(2,1)S(1)}, bf16[48,100,232]{2,0,1:T(8,128)(2,1)}, u32[]{:S(2)}) copy-start(bf16[48,100,232]{2,0,1:T(8,128)(2,1)} %param.12) | copy-start | bytes 6681604
  7.2 32.2 %copy-start.2 = (s32[384,1]{0,1:T(1,128)S(1)}, s32[384,1]{0,1:T(1,128)}, u32[]{:S(2)}) copy-start(s32[384,1]{0,1:T(1,128)} %param.21) | copy-start | bytes 4612
  7.2 52.9 %all-gather.2.cloned.1.call-start = ((), (), s32[]{:S(2)}) async-start(), calls=%async_computation.4 | async-start | bytes 2297856 | tf_op jit(solution)/shard_map/all_gather | solution.py:330
  40.7 27.6 %all-to-all-start.2 = ((bf16[16,24,384]{2,1,0:T(8,128)(2,1)}), bf16[16,24,384]{2,1,0:T(8,128)(2,1)S(1)}, u32[]{:S(2)}, u32[]{:S(2)}) async-start(bf16[16,24,384]{2,1,0:T(8,128)(2,1)} %shard_map.134), calls=%async_computation.2 | async-start | bytes 589824 | tf_op jit(solution)/shard_map/all_to_all | solution.py:341
  60.1 12.5 %copy-start.1 = (f32[384,8]{0,1:T(8,128)S(1)}, f32[384,8]{0,1:T(8,128)}, u32[]{:S(2)}) copy-start(f32[384,8]{0,1:T(8,128)} %param.20) | copy-start | bytes 36868
  68.3 16.0 %all-to-all-start = ((bf16[16,24,384]{2,1,0:T(8,128)(2,1)}), bf16[16,24,384]{2,1,0:T(8,128)(2,1)S(1)}, u32[]{:S(2)}, u32[]{:S(2)}) async-start(bf16[16,24,384]{2,1,0:T(8,128)(2,1)} %get-tuple-element.14), calls=%async_computation | async-start | bytes 589824 | tf_op jit(solution)/shard_map/all_to_all | solution.py:368
  72.6 1.0 copy-start.3
  73.6 0.8 copy-start.4
  74.4 0.7 copy-start.5
  76.8 3.3 %collective-permute-start = (bf16[8,24,384]{2,1,0:T(8,128)(2,1)S(1)}, bf16[8,24,384]{2,1,0:T(8,128)(2,1)S(1)}, u32[]{:S(2)}, u32[]{:S(2)}) collective-permute-start(bf16[8,24,384]{2,1,0:T(8,128)(2,1)S(1)} %get-tuple-element.19), channel_id=1, source_target_pairs={{0,1},{1,0},{2,3},{3,2},{4,5},{5,4},{6,7},{7,6},{8,9},{9,8},{10,11... | collective-permute-start | bytes 442376 | tf_op jit(solution)/shard_map/ppermute | solution.py:385
  80.1 8.0 %collective-permute-start.1 = (bf16[8,24,384]{2,1,0:T(8,128)(2,1)S(1)}, bf16[8,24,384]{2,1,0:T(8,128)(2,1)S(1)}, u32[]{:S(2)}, u32[]{:S(2)}) collective-permute-start(bf16[8,24,384]{2,1,0:T(8,128)(2,1)S(1)} %shard_map.136), channel_id=1, source_target_pairs={{0,2},{1,3},{2,0},{3,1},{4,6},{5,7},{6,4},{7,5},{8,10},{9,11},{10,... | collective-permute-start | bytes 442376 | tf_op jit(solution)/shard_map/ppermute | solution.py:385
  88.1 36.2 %all-to-all-start.3 = ((bf16[32,24,384]{2,1,0:T(8,128)(2,1)}), bf16[32,24,384]{2,1,0:T(8,128)(2,1)S(1)}, u32[]{:S(2)}, u32[]{:S(2)}) async-start(bf16[32,24,384]{2,1,0:T(8,128)(2,1)} %bitcast.9), calls=%async_computation.3 | async-start | bytes 1179648 | tf_op jit(solution)/shard_map/all_to_all | solution.py:397
  99.0 10.7 %collective-permute-start.2 = (bf16[8,24,384]{2,1,0:T(8,128)(2,1)S(1)}, bf16[8,24,384]{2,1,0:T(8,128)(2,1)S(1)}, u32[]{:S(2)}, u32[]{:S(2)}) collective-permute-start(bf16[8,24,384]{2,1,0:T(8,128)(2,1)S(1)} %shard_map.137), channel_id=1, source_target_pairs={{0,4},{1,5},{2,6},{3,7},{4,0},{5,1},{6,2},{7,3},{8,12},{9,13},{10,... | collective-permute-start | bytes 442376 | tf_op jit(solution)/shard_map/ppermute | solution.py:385
  109.7 13.9 %collective-permute-start.3 = (bf16[8,24,384]{2,1,0:T(8,128)(2,1)S(1)}, bf16[8,24,384]{2,1,0:T(8,128)(2,1)S(1)}, u32[]{:S(2)}, u32[]{:S(2)}) collective-permute-start(bf16[8,24,384]{2,1,0:T(8,128)(2,1)S(1)} %shard_map.138), channel_id=1, source_target_pairs={{0,8},{1,9},{2,10},{3,11},{4,12},{5,13},{6,14},{7,15},{8,0},{9,1},... | collective-permute-start | bytes 442376 | tf_op jit(solution)/shard_map/ppermute | solution.py:385
Sparse Core Ops, SparseCore 0:
  10.7 49.3 all-gather.1

commit v4 on v3

--- a/solution.py
+++ b/solution.py
@@ -108,29 +108,28 @@
 
 def trunk_kernel(
     plan, n_tokens,
-    ids, cells_ref, film, learner, packed,
-    tokens_out, mixed_out, attend_out, scale_out,
-    w, e, d, h, wd, exw, sems,
+    ids, own, table, learner_in, packed,
+    tokens_out, carry_out,
+    w, e, d, h, wd, exw, cells_ref, film, learner, sems,
 ):
     exp, sq, ex, dep = plan
     width = film.shape[2]
     hidden = packed.shape[0]
-    late, early = (
-        pltpu.make_async_copy(packed.at[:, lanes], w.at[:, lanes], sems.at[k])
-        for k, lanes in enumerate((pl.ds(0, width), pl.ds(width, LANES - width)))
-    )
-    early.start()
-    late.start()
     bands = GRID
     rows = bands * BAND
     n_frames = 3
     first = lax.axis_index("mp") * n_frames
-    scales, shifts = [], []
-    for f in range(n_frames):
-        name = ids[first + f]
-        row = film[name]
-        scales.append(1.0 + row[0:1, :])
-        shifts.append(row[1:2, :])
+    front, back = pl.ds(0, width), pl.ds(width, LANES - width)
+    pairs = [(packed.at[:, back], w.at[:, back]), (own, cells_ref), (learner_in, learner)]
+    pairs += [(table.at[ids[first + f]], film.at[f]) for f in range(n_frames)]
+    pairs += [(packed.at[:, front], w.at[:, front])]
+    moves = [pltpu.make_async_copy(a, b, sems.at[k]) for k, (a, b) in enumerate(pairs)]
+    for move in moves:
+        move.start()
+    for move in moves[:-1]:
+        move.wait()
+    scales = [1.0 + film[f, 0:1, :] for f in range(n_frames)]
+    shifts = [film[f, 1:2, :] for f in range(n_frames)]
 
     def by_band(parts):
         frame = iota((BAND, parts[0].shape[1]), 0) % n_frames
@@ -138,12 +137,12 @@
 
     scale_band = by_band(scales)
     shift_band = by_band(shifts)
-    scale_out[...] = jnp.concatenate(scales + [jnp.zeros((8 - n_frames, width), f32)], axis=0)
+    scale_out = jnp.concatenate(scales + [jnp.zeros((8 - n_frames, width), f32)], axis=0)
+    carry_out[rows + n_frames * n_tokens:, :] = scale_out
     pick = (iota((16, LANES - TAIL), 1) == iota((16, LANES - TAIL), 0) + dep) | (
         iota((16, LANES - TAIL), 1) == iota((16, LANES - TAIL), 0) + dep + KS * KS
     )
     pick = onehot(pick & (iota((16, LANES - TAIL), 0) < KS * KS))
-    early.wait()
     wd[...] = dot(pick, w[:, TAIL:LANES], NT)
     e[...] = dot(cells_ref[...], w[:, exp:exp + 256], NT)
     place = iota((BAND, 128), 0)
@@ -202,18 +201,18 @@
     for r in range(bands):
         band = slice(r * BAND, (r + 1) * BAND)
         h[band, :] = (d[band, :] * exw[...]).astype(bf16)
-    late.wait()
+    moves[-1].wait()
     block = dot(h[...], w[:, 0:width])
     mixed = (
         block.reshape(bands, BAND, width) * scale_band[None] + shift_band[None]
     ).reshape(rows, width)
-    mixed_out[...] = mixed
+    carry_out[0:rows, :] = mixed
     tiled = jnp.concatenate([learner[...]] * n_frames, axis=0)
     logits = dot(tiled, mixed, NT, highest)
     at = iota(logits.shape, 1) % BAND
     mine = (at % n_frames == iota(logits.shape, 0) // n_tokens) & (at < BAND - 2)
     attend = jnp.where(mine, sigmoid(logits), 0.0)
-    attend_out[...] = attend
+    carry_out[rows:rows + n_frames * n_tokens, 0:rows] = attend
     tokens = dot(attend, mixed, precision=highest) * (1.0 / (GRID * GRID))
     tokens = tokens.astype(bf16)
     for k in range(tokens_out.shape[0]):
@@ -230,7 +229,8 @@
     return onehot(iota((peers * capacity, count), 0) == slot)
 
 
-def scatter_kernel(peers, capacity, tokens, dest, out):
+def scatter_kernel(peers, capacity, tokens, dest, after, out):
+    del after
     out[...] = dot(slots_onehot(dest[...], peers, capacity), tokens[...]).astype(bf16)
 
 
@@ -241,14 +241,18 @@
         out[k] = chosen[k * each:(k + 1) * each].astype(bf16)
 
 
-def backward_kernel(n_tokens, cells, mixed, attend, scale, learner, grads, kept, sent, res):
+def backward_kernel(n_tokens, cells, carry, learner, grads, *outs):
     n_frames = 3
-    share = kept.shape[1]
+    *far, res = outs
+    share = far[0].shape[1]
+    rows = GRID * BAND
+    mixed = carry[0:rows, :]
+    held = carry[rows:rows + n_frames * n_tokens, 0:rows]
+    scale = carry[rows + n_frames * n_tokens:, :]
     grad = grads[0].astype(f32)
     for k in range(1, grads.shape[0]):
         grad = grad + grads[k].astype(f32)
-    inner = dot(grad, mixed[...], NT, highest)
-    held = attend[...]
+    inner = dot(grad, mixed, NT, highest)
     slope = inner * (1.0 / (GRID * GRID)) * held * (1.0 - held)
     both = jnp.concatenate([held * (1.0 / (GRID * GRID)), slope], axis=0)
     shape = (mixed.shape[0], n_frames * 128)
@@ -261,28 +265,34 @@
         lanes = slice(f * 128, (f + 1) * 128)
         res[:, lanes] = dot(factors * scale[f:f + 1, :], both[:, lanes], TN, highest)
     me = lax.axis_index("mp")
-    for k in range(kept.shape[0]):
-        apart = 2 * sum(((k >> bit) & 1) << (2 - bit) for bit in range(3))
-        for out, far in ((kept, apart), (sent, apart + 1)):
-            first = pl.multiple_of(lax.bitwise_xor(me, far) * share, 8)
-            out[k] = res[pl.ds(first, share), :].astype(bf16)
-
-
-def join_kernel(wanted, *refs):
-    *parts, out = refs
-    for k, (part, block) in enumerate(wanted):
-        out[k] = parts[part][block]
-
-
-def settle_kernel(wanted, *refs):
+    for k, out in enumerate(far):
+        near = out.shape[0]
+        for j in range(near):
+            first = pl.multiple_of(lax.bitwise_xor(me, near * k + j) * share, 8)
+            out[j] = res[pl.ds(first, share), :].astype(bf16)
+
+
+def join_kernel(after, *refs):
+    del after
+    parts, outs = refs[:len(refs) // 2 + 1], refs[len(refs) // 2 + 1:]
+    for j, out in enumerate(outs):
+        for k, part in enumerate(parts):
+            out[k] = part[j + 1]
+
+
+def settle_kernel(*refs):
     *parts, out = refs
     n_frames = 3
     cells = out.shape[2]
     me = lax.axis_index("mp")
-    for k, (part, block) in enumerate(wanted):
-        source = lax.bitwise_xor(me, k) * n_frames
-        for f in range(n_frames):
-            out[source + f] = parts[part][block, :, f * 128:f * 128 + cells]
+    near = parts[0].shape[0]
+    far, joined = parts[:len(parts) - near + 1], parts[len(parts) - near + 1:]
+    for k in range(len(far)):
+        for j in range(near):
+            block = far[k][0] if j == 0 else joined[j - 1][k]
+            source = lax.bitwise_xor(me, near * k + j) * n_frames
+            for f in range(n_frames):
+                out[source + f] = block[:, f * 128:f * 128 + cells]
 
 
 def per_device(
@@ -340,20 +350,19 @@
     )
     grads = lax.all_to_all(picked, "mp", split_axis=0, concat_axis=0, tiled=True)
 
+    packed, grads = lax.optimization_barrier((packed, grads))
     own = lax.dynamic_slice_in_dim(frames, lax.axis_index("mp") * n_frames, n_frames, 0)
     own = own.transpose(1, 0, 2).reshape(GRID, GRID * n_frames, c_in)
     own = jnp.pad(own, ((0, 0), (0, BAND - GRID * n_frames), (0, 256 - c_in)))
     own = own.reshape(rows, 256)
-    copies, mixed, attend, scale = call(
+    copies, carry = call(
         functools.partial(trunk_kernel, plan, n_tokens),
         (
             sds((n_mp, n_frames * n_tokens, width), bf16),
-            sds((rows, width), f32),
-            sds((n_frames * n_tokens, rows), f32),
-            sds((8, width), f32),
+            sds((rows + n_frames * n_tokens + 8, width), f32),
         ),
         instr_ids, own, film_table, learner, packed,
-        in_specs=[pl.BlockSpec(memory_space=pltpu.SMEM)] + [vmem] * 3 + [pl.BlockSpec(memory_space=pl.ANY)],
+        in_specs=[pl.BlockSpec(memory_space=pltpu.SMEM)] + [pl.BlockSpec(memory_space=pl.ANY)] * 4,
         scratch=[
             pltpu.VMEM((hidden, LANES), bf16),
             pltpu.VMEM((rows, hidden), f32),
@@ -361,46 +370,43 @@
             pltpu.VMEM((rows, hidden), bf16),
             pltpu.VMEM((16, hidden), f32),
             pltpu.VMEM((BAND, hidden), f32),
-            pltpu.SemaphoreType.DMA((2,)),
+            pltpu.VMEM((rows, 256), bf16),
+            pltpu.VMEM((n_frames, 2, width), f32),
+            pltpu.VMEM((n_tokens, width), f32),
+            pltpu.SemaphoreType.DMA((4 + n_frames,)),
         ],
         flops=2e9, moved=3e7, vmem=58,
     )
     tokens = lax.all_to_all(copies, "mp", split_axis=0, concat_axis=0, tiled=True)
+    near = 4
+    blocks = sds((near, share, n_frames * 128), bf16)
+    parts = call(
+        functools.partial(backward_kernel, n_tokens, cells),
+        (blocks,) * (n_mp // near),
+        carry, learner, grads,
+        scratch=[pltpu.VMEM((width, n_frames * 128), f32)],
+        flops=1e9, moved=2e6,
+    )
+
+    def swap(value, far):
+        return lax.ppermute(value, "mp", [(m, m ^ far) for m in range(n_mp)]) if far else value
+
+    parts = [swap(part, near * k) for k, part in enumerate(parts)]
     outgoing = call(
         functools.partial(scatter_kernel, peers, capacity),
         sds((peers * capacity, width), bf16),
-        tokens.reshape(count * n_tokens, width), dest,
+        tokens.reshape(count * n_tokens, width), dest, parts[2],
+        in_specs=[vmem, vmem, pl.BlockSpec(memory_space=pl.ANY)],
         flops=3e8, moved=2e6,
     )
-    blocks = sds((n_mp // 2, share, n_frames * 128), bf16)
-    kept, sent = call(
-        functools.partial(backward_kernel, n_tokens, cells),
-        (blocks, blocks),
-        mixed, attend, scale, learner, grads,
-        scratch=[pltpu.VMEM((width, n_frames * 128), f32)],
-        flops=1e9, moved=2e6,
-    )
-
-    def swap(value, bit):
-        return lax.ppermute(value, "mp", [(m, m ^ bit) for m in range(n_mp)])
-
-    parts = [kept, swap(sent, 1)]
-    groups = [(0, 0), (1, 0)]
-    for step, bit in enumerate((2, 4, 8)):
-        held = 4 >> step
-        if bit == 4:
-            outgoing, *parts = lax.optimization_barrier((outgoing, *parts))
-        wanted = [(p, first + held + k) for p, first in groups for k in range(held)]
-        sent = call(functools.partial(join_kernel, wanted), blocks, *parts)
-        groups = groups + [(len(parts), held * k) for k in range(len(groups))]
-        parts = parts + [swap(sent, bit)]
+    joined = call(join_kernel, (blocks,) * (near - 1), outgoing, *parts,
+                  in_specs=[pl.BlockSpec(memory_space=pl.ANY)] + [vmem] * len(parts))
+    joined = [swap(part, j + 1) for j, part in enumerate(joined)]
     rows_in = lax.all_to_all(
         outgoing.reshape(peers, capacity, width), "seq", split_axis=0, concat_axis=0, tiled=True
     )
-    feature_grad = call(
-        functools.partial(settle_kernel, groups), sds((count, share, cells), bf16), *parts
-    )
-    w_policy, feature_grad = lax.optimization_barrier((w_policy, feature_grad))
+    feature_grad = call(settle_kernel, sds((count, share, cells), bf16), *parts, *joined)
+    rows_in, feature_grad = lax.optimization_barrier((rows_in, feature_grad))
     policy_in = dot(rows_in.reshape(peers * capacity, width), w_policy).astype(bf16)
 
     feature_grad = feature_grad.transpose(0, 2, 1)

time: 135 us -> 135 us (level)
  starting transfers between devices: 43.4 us -> 47.2 us
  waiting for transfers between devices: 24.4 us -> 21.6 us
  local copies, waits for them, and re-layouts: 3.48 us -> 2.03 us
    all_to_all x1, waiting for transfers between devices: 0.01 us -> 11.1 us  [per_device(): lax.all_to_all(picked, 'mp', split_axis=0, concat_axis=0, tiled=True)]
    all_gather x1, waiting for transfers between devices: 7.91 us -> 0.01 us  [per_device(): packed = lax.all_gather(mine, 'mp', axis=0, tiled=True)]
    ppermute x4 -> x6, waiting for transfers between devices: 16.1 us -> 10.5 us  [swap(): lax.ppermute(value, 'mp', [(m, m ^ far) for m in range(n_mp)])]
    ppermute x4 -> x6, starting transfers between devices: 17.8 us -> 23.2 us  [swap(): lax.ppermute(value, 'mp', [(m, m ^ far) for m in range(n_mp)])]
    unnamed x12 -> x8, local copies, waits for them, and re-layouts: 2.52 us -> 1.06 us
    pallas_call x9 -> x7, Pallas kernels: 15.7 us -> 15.5 us  [call(): pl.pallas_call(kernel, out_shape=out_shape, in_specs=in_specs or [pl.Bloc...]
  transfers between devices with their start and end apart: 8 -> 10, of which waited for: 6 -> 5; matrix products, arithmetic and copies ran while one was open for 2% -> 2% of each run, Pallas kernels for 10% -> 3%
where the time goes in v4:
time: 135 us; the launch traced here: 133 us
  starting transfers between devices  47.2 us (35%)
  blocking collectives  28.2 us (21%)
  waiting for transfers between devices  21.6 us (16%)
  Pallas kernels  15.5 us (11%)
  between operations  14.2 us (11%)
  matrix products  4.44 us (3%)
  local copies, waits for them, and re-layouts  2.03 us (2%)
    all_to_all x1, blocking collectives, per_device(): lax.all_to_all(grad_part.reshape(peers, capacity, width), 'seq', split_ax...  28.2 us
    ppermute x6, starting transfers between devices, swap(): lax.ppermute(value, 'mp', [(m, m ^ far) for m in range(n_mp)])  23.2 us
    pallas_call x7, Pallas kernels, call(): pl.pallas_call(kernel, out_shape=out_shape, in_specs=in_specs or [pl.Bloc...  15.5 us
    all_to_all x1, waiting for transfers between devices, per_device(): lax.all_to_all(picked, 'mp', split_axis=0, concat_axis=0, tiled=True)  11.1 us
    ppermute x6, waiting for transfers between devices, swap(): lax.ppermute(value, 'mp', [(m, m ^ far) for m in range(n_mp)])  10.5 us
    all_to_all x1, starting transfers between devices, per_device(): lax.all_to_all(picked, 'mp', split_axis=0, concat_axis=0, tiled=True)  10.4 us
    all_to_all x1, starting transfers between devices, per_device(): lax.all_to_all(outgoing.reshape(peers, capacity, width), 'seq', split_axi...  10 us
    dot_general x2, matrix products, dot(): lax.dot_general(a, b, dims, precision=precision, preferred_element_type=f32)  4.44 us
  transfers between devices with their start and end apart: 10, of which 5 were waited for; matrix products, arithmetic and copies ran while one was open for 2% of the time, Pallas kernels for 3%

profile of v4, /device:TPU:6, one launch (start us, length us, event | category | flops | bytes accessed | tf_op | source)
XLA Modules:
  0.0 133.3 jit_solution(17315638528495659508)
XLA Ops:
  7.2 2.0 %shard_map.131 = bf16[88,768]{1,0:T(8,128)(2,1)} custom-call(bf16[87,232]{1,0:T(8,128)(2,1)} %bitcast.26, bf16[87,384]{1,0:T(8,128)(2,1)} %project_in.1, f32[58,87]{1,0:T(8,128)} %bitcast.27, f32[58,87]{1,0:T(8,128)} %excite_in.1, f32[9,87]{1,0:T(8,128)} %depth_in.1), custom_call_target="tpu_custom_call" | custom-call | flops 1000000 | bytes 1000000 | tf_op jit(solution)/shard_map/pallas_call | solution.py:54
  9.3 1.8 %convolution_convert_fusion.1 = bf16[768,384]{1,0:T(8,128)(2,1)S(1)} fusion(bf16[768,512]{1,0:T(8,128)(2,1)} %param.23, bf16[384,512]{1,0:T(8,128)(2,1)} %param.22), kind=kOutput, calls=%fused_computation.1 | convolution fusion | flops 302284800 | bytes 1769472 | tf_op jit(solution)/shard_map/dot_general | solution.py:28
  11.1 28.2 %all_to_all.20 = bf16[32,24,384]{2,1,0:T(8,128)(2,1)S(1)} all-to-all(bf16[32,24,384]{2,1,0:T(8,128)(2,1)S(1)} %bitcast.23), channel_id=1, replica_groups=mesh['seq'=32,'mp'=16] {'seq'}, dimensions={0} | all-to-all | bytes 1179648 | tf_op jit(solution)/shard_map/all_to_all | solution.py:342
  39.3 1.4 %shard_map.132 = bf16[16,24,384]{2,1,0:T(8,128)(2,1)} custom-call(bf16[768,384]{1,0:T(8,128)(2,1)S(1)} %bitcast.17, s32[1,384]{1,0:T(1,128)S(1)} %bitcast.21), custom_call_target="tpu_custom_call" | custom-call | flops 300000000 | bytes 2000000 | tf_op jit(solution)/shard_map/pallas_call | solution.py:54
  40.7 10.4 %all-to-all-start.1 = ((bf16[16,24,384]{2,1,0:T(8,128)(2,1)}), bf16[16,24,384]{2,1,0:T(8,128)(2,1)S(1)}, u32[]{:S(2)}, u32[]{:S(2)}) async-start(bf16[16,24,384]{2,1,0:T(8,128)(2,1)} %shard_map.132), calls=%async_computation.1 | async-start | bytes 589824 | tf_op jit(solution)/shard_map/all_to_all | solution.py:351
  52.2 11.1 %all-to-all-done.1.grads = bf16[16,24,384]{2,1,0:T(8,128)(2,1)S(1)} async-done(((bf16[16,24,384]{2,1,0:T(8,128)(2,1)}), bf16[16,24,384]{2,1,0:T(8,128)(2,1)S(1)}, u32[]{:S(2)}, u32[]{:S(2)}) %all-to-all-start.1) | async-done | bytes 294944 | tf_op jit(solution)/shard_map/all_to_all | solution.py:351
  63.3 8.1 %shard_map.133 = (bf16[16,24,384]{2,1,0:T(8,128)(2,1)}, f32[352,384]{1,0:T(8,128)}) custom-call(s32[48]{0:T(128)} %ids.1, bf16[320,256]{1,0:T(8,128)(2,1)} %bitcast.25, f32[64,2,384]{2,1,0:T(2,128)} %table.1, f32[8,384]{1,0:T(8,128)} %bitcast.19, bf16[1408,768]{1,0:T(8,128)(2,1)} %all-gather.2.cloned.1.call-done.packed), custom_call_target="tpu_custom_call" | custom-call | flops 2000000000 | bytes 30000000 | tf_op jit(solution)/shard_map/pallas_call | solution.py:54
  71.3 3.5 %all-to-all-start.2 = ((bf16[16,24,384]{2,1,0:T(8,128)(2,1)}), bf16[16,24,384]{2,1,0:T(8,128)(2,1)S(1)}, u32[]{:S(2)}, u32[]{:S(2)}) async-start(bf16[16,24,384]{2,1,0:T(8,128)(2,1)} %get-tuple-element.16), calls=%async_computation.2 | async-start | bytes 589824 | tf_op jit(solution)/shard_map/all_to_all | solution.py:380
  74.9 1.0 copy-done.3
  75.9 1.7 %shard_map.134 = (bf16[4,24,384]{2,1,0:T(8,128)(2,1)S(1)}, bf16[4,24,384]{2,1,0:T(8,128)(2,1)S(1)}, bf16[4,24,384]{2,1,0:T(8,128)(2,1)S(1)}, bf16[4,24,384]{2,1,0:T(8,128)(2,1)S(1)}) custom-call(f32[352,384]{1,0:T(8,128)S(1)} %copy-done.3, f32[8,384]{1,0:T(8,128)S(1)} %bitcast.20, bf16[16,24,384]{2,1,0:T(8,128)(2,1)S(1)} %all-to-all-done.1.grads), custom_call_target="tpu_custom_call" | custom-call | flops 1000000000 | bytes 2000000 | tf_op jit(solution)/shard_map/pallas_call | solution.py:54
  77.7 7.7 %collective-permute-start = (bf16[4,24,384]{2,1,0:T(8,128)(2,1)S(1)}, bf16[4,24,384]{2,1,0:T(8,128)(2,1)S(1)}, u32[]{:S(2)}, u32[]{:S(2)}) collective-permute-start(bf16[4,24,384]{2,1,0:T(8,128)(2,1)S(1)} %get-tuple-element.19), channel_id=1, source_target_pairs={{0,8},{1,9},{2,10},{3,11},{4,12},{5,13},{6,14},{7,15},{8,0},{9,1},... | collective-permute-start | bytes 221192 | tf_op jit(solution)/shard_map/ppermute | solution.py:392
  85.4 4.4 %collective-permute-done.after.refs_2_ = bf16[4,24,384]{2,1,0:T(8,128)(2,1)S(1)} collective-permute-done((bf16[4,24,384]{2,1,0:T(8,128)(2,1)S(1)}, bf16[4,24,384]{2,1,0:T(8,128)(2,1)S(1)}, u32[]{:S(2)}, u32[]{:S(2)}) %collective-permute-start) | collective-permute-done | bytes 73760 | tf_op jit(solution)/shard_map/ppermute | solution.py:392
  89.8 1.5 %shard_map.135.after = bf16[768,384]{1,0:T(8,128)(2,1)} custom-call(bf16[384,384]{1,0:T(8,128)(2,1)S(1)} %bitcast.18, s32[1,384]{1,0:T(1,128)S(1)} %bitcast.22, bf16[4,24,384]{2,1,0:T(8,128)(2,1)S(1)} %collective-permute-done.after.refs_2_), custom_call_target="tpu_custom_call" | custom-call | flops 300000000 | bytes 2000000 | tf_op jit(solution)/shard_map/pallas_call | solution.py:54
  91.3 10.0 %all-to-all-start.3 = ((bf16[32,24,384]{2,1,0:T(8,128)(2,1)}), bf16[32,24,384]{2,1,0:T(8,128)(2,1)}, u32[]{:S(2)}, u32[]{:S(2)}) async-start(bf16[32,24,384]{2,1,0:T(8,128)(2,1)} %bitcast.9), calls=%async_computation.3 | async-start | bytes 1179648 | tf_op jit(solution)/shard_map/all_to_all | solution.py:405
  101.3 2.9 %collective-permute-start.1 = (bf16[4,24,384]{2,1,0:T(8,128)(2,1)S(1)}, bf16[4,24,384]{2,1,0:T(8,128)(2,1)S(1)}, u32[]{:S(2)}, u32[]{:S(2)}) collective-permute-start(bf16[4,24,384]{2,1,0:T(8,128)(2,1)S(1)} %get-tuple-element.21), channel_id=1, source_target_pairs={{0,4},{1,5},{2,6},{3,7},{4,0},{5,1},{6,2},{7,3},{8,12},{9,13},{10,... | collective-permute-start | bytes 221192 | tf_op jit(solution)/shard_map/ppermute | solution.py:392
  104.3 5.0 %collective-permute-start.2 = (bf16[4,24,384]{2,1,0:T(8,128)(2,1)S(1)}, bf16[4,24,384]{2,1,0:T(8,128)(2,1)S(1)}, u32[]{:S(2)}, u32[]{:S(2)}) collective-permute-start(bf16[4,24,384]{2,1,0:T(8,128)(2,1)S(1)} %get-tuple-element.22), channel_id=1, source_target_pairs={{0,12},{1,13},{2,14},{3,15},{4,8},{5,9},{6,10},{7,11},{8,4},{9,5},... | collective-permute-start | bytes 221192 | tf_op jit(solution)/shard_map/ppermute | solution.py:392
  109.3 3.3 %collective-permute-done.2.refs_3_ = bf16[4,24,384]{2,1,0:T(8,128)(2,1)S(1)} collective-permute-done((bf16[4,24,384]{2,1,0:T(8,128)(2,1)S(1)}, bf16[4,24,384]{2,1,0:T(8,128)(2,1)S(1)}, u32[]{:S(2)}, u32[]{:S(2)}) %collective-permute-start.2) | collective-permute-done | bytes 73760 | tf_op jit(solution)/shard_map/ppermute | solution.py:392
  112.6 1.9 %collective-permute-start.3 = (bf16[4,24,384]{2,1,0:T(8,128)(2,1)S(1)}, bf16[4,24,384]{2,1,0:T(8,128)(2,1)S(1)}, u32[]{:S(2)}, u32[]{:S(2)}) collective-permute-start(bf16[4,24,384]{2,1,0:T(8,128)(2,1)S(1)} %get-tuple-element.23), channel_id=1, source_target_pairs={{0,1},{1,0},{2,3},{3,2},{4,5},{5,4},{6,7},{7,6},{8,9},{9,8},{10,11... | collective-permute-start | bytes 221192 | tf_op jit(solution)/shard_map/ppermute | solution.py:392
  114.6 2.3 %collective-permute-start.4 = (bf16[4,24,384]{2,1,0:T(8,128)(2,1)S(1)}, bf16[4,24,384]{2,1,0:T(8,128)(2,1)S(1)}, u32[]{:S(2)}, u32[]{:S(2)}) collective-permute-start(bf16[4,24,384]{2,1,0:T(8,128)(2,1)S(1)} %get-tuple-element.24), channel_id=1, source_target_pairs={{0,2},{1,3},{2,0},{3,1},{4,6},{5,7},{6,4},{7,5},{8,10},{9,11},{10,... | collective-permute-start | bytes 221192 | tf_op jit(solution)/shard_map/ppermute | solution.py:392
  116.9 3.3 %collective-permute-start.5 = (bf16[4,24,384]{2,1,0:T(8,128)(2,1)S(1)}, bf16[4,24,384]{2,1,0:T(8,128)(2,1)S(1)}, u32[]{:S(2)}, u32[]{:S(2)}) collective-permute-start(bf16[4,24,384]{2,1,0:T(8,128)(2,1)S(1)} %get-tuple-element.25), channel_id=1, source_target_pairs={{0,3},{1,2},{2,1},{3,0},{4,7},{5,6},{6,5},{7,4},{8,11},{9,10},{10,... | collective-permute-start | bytes 221192 | tf_op jit(solution)/shard_map/ppermute | solution.py:392
  120.3 0.9 collective-permute-done.4.refs_5_
  121.1 1.9 %collective-permute-done.5.refs_6_ = bf16[4,24,384]{2,1,0:T(8,128)(2,1)S(1)} collective-permute-done((bf16[4,24,384]{2,1,0:T(8,128)(2,1)S(1)}, bf16[4,24,384]{2,1,0:T(8,128)(2,1)S(1)}, u32[]{:S(2)}, u32[]{:S(2)}) %collective-permute-start.5) | collective-permute-done | bytes 73760 | tf_op jit(solution)/shard_map/ppermute | solution.py:392
  123.1 0.8 shard_map.137
  123.8 2.6 %convolution_convert_fusion = bf16[768,512]{1,0:T(8,128)(2,1)} fusion(bf16[768,384]{1,0:T(8,128)(2,1)} %bitcast.10, bf16[384,512]{1,0:T(8,128)(2,1)} %param.22), kind=kOutput, calls=%fused_computation | convolution fusion | flops 302383104 | bytes 1769472 | tf_op jit(solution)/shard_map/dot_general | solution.py:28
  (18 shorter events, 1.1 us)
Async XLA Ops:
  7.2 44.0 %copy-start = (bf16[48,100,232]{2,0,1:T(8,128)(2,1)S(1)}, bf16[48,100,232]{2,0,1:T(8,128)(2,1)}, u32[]{:S(2)}) copy-start(bf16[48,100,232]{2,0,1:T(8,128)(2,1)} %param.12) | copy-start | bytes 6681604
  7.2 32.2 %copy-start.2 = (s32[384,1]{0,1:T(1,128)S(1)}, s32[384,1]{0,1:T(1,128)}, u32[]{:S(2)}) copy-start(s32[384,1]{0,1:T(1,128)} %param.21) | copy-start | bytes 4612
  7.2 56.1 %all-gather.2.cloned.1.call-start = ((), (), s32[]{:S(2)}) async-start(), calls=%async_computation.4 | async-start | bytes 2297856 | tf_op jit(solution)/shard_map/all_gather | solution.py:340
  40.7 22.5 %all-to-all-start.1 = ((bf16[16,24,384]{2,1,0:T(8,128)(2,1)}), bf16[16,24,384]{2,1,0:T(8,128)(2,1)S(1)}, u32[]{:S(2)}, u32[]{:S(2)}) async-start(bf16[16,24,384]{2,1,0:T(8,128)(2,1)} %shard_map.132), calls=%async_computation.1 | async-start | bytes 589824 | tf_op jit(solution)/shard_map/all_to_all | solution.py:351
  63.3 11.6 %copy-start.1 = (f32[384,8]{0,1:T(8,128)S(1)}, f32[384,8]{0,1:T(8,128)}, u32[]{:S(2)}) copy-start(f32[384,8]{0,1:T(8,128)} %param.20) | copy-start | bytes 36868
  71.3 18.4 %all-to-all-start.2 = ((bf16[16,24,384]{2,1,0:T(8,128)(2,1)}), bf16[16,24,384]{2,1,0:T(8,128)(2,1)S(1)}, u32[]{:S(2)}, u32[]{:S(2)}) async-start(bf16[16,24,384]{2,1,0:T(8,128)(2,1)} %get-tuple-element.16), calls=%async_computation.2 | async-start | bytes 589824 | tf_op jit(solution)/shard_map/all_to_all | solution.py:380
  74.9 1.1 copy-start.3
  77.7 12.1 %collective-permute-start = (bf16[4,24,384]{2,1,0:T(8,128)(2,1)S(1)}, bf16[4,24,384]{2,1,0:T(8,128)(2,1)S(1)}, u32[]{:S(2)}, u32[]{:S(2)}) collective-permute-start(bf16[4,24,384]{2,1,0:T(8,128)(2,1)S(1)} %get-tuple-element.19), channel_id=1, source_target_pairs={{0,8},{1,9},{2,10},{3,11},{4,12},{5,13},{6,14},{7,15},{8,0},{9,1},... | collective-permute-start | bytes 221192 | tf_op jit(solution)/shard_map/ppermute | solution.py:392
  91.3 32.6 %all-to-all-start.3 = ((bf16[32,24,384]{2,1,0:T(8,128)(2,1)}), bf16[32,24,384]{2,1,0:T(8,128)(2,1)}, u32[]{:S(2)}, u32[]{:S(2)}) async-start(bf16[32,24,384]{2,1,0:T(8,128)(2,1)} %bitcast.9), calls=%async_computation.3 | async-start | bytes 1179648 | tf_op jit(solution)/shard_map/all_to_all | solution.py:405
  101.3 8.0 %collective-permute-start.1 = (bf16[4,24,384]{2,1,0:T(8,128)(2,1)S(1)}, bf16[4,24,384]{2,1,0:T(8,128)(2,1)S(1)}, u32[]{:S(2)}, u32[]{:S(2)}) collective-permute-start(bf16[4,24,384]{2,1,0:T(8,128)(2,1)S(1)} %get-tuple-element.21), channel_id=1, source_target_pairs={{0,4},{1,5},{2,6},{3,7},{4,0},{5,1},{6,2},{7,3},{8,12},{9,13},{10,... | collective-permute-start | bytes 221192 | tf_op jit(solution)/shard_map/ppermute | solution.py:392
  104.3 8.4 %collective-permute-start.2 = (bf16[4,24,384]{2,1,0:T(8,128)(2,1)S(1)}, bf16[4,24,384]{2,1,0:T(8,128)(2,1)S(1)}, u32[]{:S(2)}, u32[]{:S(2)}) collective-permute-start(bf16[4,24,384]{2,1,0:T(8,128)(2,1)S(1)} %get-tuple-element.22), channel_id=1, source_target_pairs={{0,12},{1,13},{2,14},{3,15},{4,8},{5,9},{6,10},{7,11},{8,4},{9,5},... | collective-permute-start | bytes 221192 | tf_op jit(solution)/shard_map/ppermute | solution.py:392
  112.6 7.6 %collective-permute-start.3 = (bf16[4,24,384]{2,1,0:T(8,128)(2,1)S(1)}, bf16[4,24,384]{2,1,0:T(8,128)(2,1)S(1)}, u32[]{:S(2)}, u32[]{:S(2)}) collective-permute-start(bf16[4,24,384]{2,1,0:T(8,128)(2,1)S(1)} %get-tuple-element.23), channel_id=1, source_target_pairs={{0,1},{1,0},{2,3},{3,2},{4,5},{5,4},{6,7},{7,6},{8,9},{9,8},{10,11... | collective-permute-start | bytes 221192 | tf_op jit(solution)/shard_map/ppermute | solution.py:392
  114.6 6.6 %collective-permute-start.4 = (bf16[4,24,384]{2,1,0:T(8,128)(2,1)S(1)}, bf16[4,24,384]{2,1,0:T(8,128)(2,1)S(1)}, u32[]{:S(2)}, u32[]{:S(2)}) collective-permute-start(bf16[4,24,384]{2,1,0:T(8,128)(2,1)S(1)} %get-tuple-element.24), channel_id=1, source_target_pairs={{0,2},{1,3},{2,0},{3,1},{4,6},{5,7},{6,4},{7,5},{8,10},{9,11},{10,... | collective-permute-start | bytes 221192 | tf_op jit(solution)/shard_map/ppermute | solution.py:392
  116.9 6.1 %collective-permute-start.5 = (bf16[4,24,384]{2,1,0:T(8,128)(2,1)S(1)}, bf16[4,24,384]{2,1,0:T(8,128)(2,1)S(1)}, u32[]{:S(2)}, u32[]{:S(2)}) collective-permute-start(bf16[4,24,384]{2,1,0:T(8,128)(2,1)S(1)} %get-tuple-element.25), channel_id=1, source_target_pairs={{0,3},{1,2},{2,1},{3,0},{4,7},{5,6},{6,5},{7,4},{8,11},{9,10},{10,... | collective-permute-start | bytes 221192 | tf_op jit(solution)/shard_map/ppermute | solution.py:392
Sparse Core Ops, SparseCore 0:
  10.7 49.2 all-gather.1

commit v5 on v4

--- a/solution.py
+++ b/solution.py
@@ -108,10 +108,11 @@
 
 def trunk_kernel(
     plan, n_tokens,
-    ids, own, table, learner_in, packed,
+    ids, own, table, learner_in, packed, after,
     tokens_out, carry_out,
     w, e, d, h, wd, exw, cells_ref, film, learner, sems,
 ):
+    del after
     exp, sq, ex, dep = plan
     width = film.shape[2]
     hidden = packed.shape[0]
@@ -350,7 +351,6 @@
     )
     grads = lax.all_to_all(picked, "mp", split_axis=0, concat_axis=0, tiled=True)
 
-    packed, grads = lax.optimization_barrier((packed, grads))
     own = lax.dynamic_slice_in_dim(frames, lax.axis_index("mp") * n_frames, n_frames, 0)
     own = own.transpose(1, 0, 2).reshape(GRID, GRID * n_frames, c_in)
     own = jnp.pad(own, ((0, 0), (0, BAND - GRID * n_frames), (0, 256 - c_in)))
@@ -361,8 +361,8 @@
             sds((n_mp, n_frames * n_tokens, width), bf16),
             sds((rows + n_frames * n_tokens + 8, width), f32),
         ),
-        instr_ids, own, film_table, learner, packed,
-        in_specs=[pl.BlockSpec(memory_space=pltpu.SMEM)] + [pl.BlockSpec(memory_space=pl.ANY)] * 4,
+        instr_ids, own, film_table, learner, packed, picked,
+        in_specs=[pl.BlockSpec(memory_space=pltpu.SMEM)] + [pl.BlockSpec(memory_space=pl.ANY)] * 5,
         scratch=[
             pltpu.VMEM((hidden, LANES), bf16),
             pltpu.VMEM((rows, hidden), f32),
@@ -395,7 +395,7 @@
     outgoing = call(
         functools.partial(scatter_kernel, peers, capacity),
         sds((peers * capacity, width), bf16),
-        tokens.reshape(count * n_tokens, width), dest, parts[2],
+        tokens.reshape(count * n_tokens, width), dest, parts[1],
         in_specs=[vmem, vmem, pl.BlockSpec(memory_space=pl.ANY)],
         flops=3e8, moved=2e6,
     )

time: 135 us -> 135 us (level)
  starting transfers between devices: 47.2 us -> 45.5 us
    all_to_all x1, waiting for transfers between devices: 11.1 us -> 0.01 us  [per_device(): lax.all_to_all(picked, 'mp', split_axis=0, concat_axis=0, tiled=True)]
    all_gather x1, waiting for transfers between devices: 0.01 us -> 7.9 us  [per_device(): packed = lax.all_gather(mine, 'mp', axis=0, tiled=True)]
    ppermute x6, waiting for transfers between devices: 10.5 us -> 14.7 us  [swap(): lax.ppermute(value, 'mp', [(m, m ^ far) for m in range(n_mp)])]
    ppermute x6, starting transfers between devices: 23.2 us -> 20 us  [swap(): lax.ppermute(value, 'mp', [(m, m ^ far) for m in range(n_mp)])]
  transfers between devices with their start and end apart: 10 -> 10, of which waited for: 5 -> 6; matrix products, arithmetic and copies ran while one was open for 2% -> 2% of each run, Pallas kernels for 3% -> 9%
where the time goes in v5:
time: 135 us; the launch traced here: 133 us
  starting transfers between devices  45.5 us (34%)
  blocking collectives  28.2 us (21%)
  waiting for transfers between devices  22.6 us (17%)
  Pallas kernels  15.5 us (11%)
  between operations  14.2 us (11%)
  matrix products  4.44 us (3%)
  local copies, waits for them, and re-layouts  2.04 us (2%)
    all_to_all x1, blocking collectives, per_device(): lax.all_to_all(grad_part.reshape(peers, capacity, width), 'seq', split_ax...  28.2 us
    ppermute x6, starting transfers between devices, swap(): lax.ppermute(value, 'mp', [(m, m ^ far) for m in range(n_mp)])  20 us
    pallas_call x7, Pallas kernels, call(): pl.pallas_call(kernel, out_shape=out_shape, in_specs=in_specs or [pl.Bloc...  15.5 us
    ppermute x6, waiting for transfers between devices, swap(): lax.ppermute(value, 'mp', [(m, m ^ far) for m in range(n_mp)])  14.7 us
    all_to_all x1, starting transfers between devices, per_device(): lax.all_to_all(outgoing.reshape(peers, capacity, width), 'seq', split_axi...  10.9 us
    all_to_all x1, starting transfers between devices, per_device(): lax.all_to_all(picked, 'mp', split_axis=0, concat_axis=0, tiled=True)  10.4 us
    all_gather x1, waiting for transfers between devices, per_device(): packed = lax.all_gather(mine, 'mp', axis=0, tiled=True)  7.9 us
    dot_general x2, matrix products, dot(): lax.dot_general(a, b, dims, precision=precision, preferred_element_type=f32)  4.44 us
  transfers between devices with their start and end apart: 10, of which 6 were waited for; matrix products, arithmetic and copies ran while one was open for 2% of the time, Pallas kernels for 9%

profile of v5, /device:TPU:6, one launch (start us, length us, event | category | flops | bytes accessed | tf_op | source)
XLA Modules:
  0.0 132.6 jit_solution(10946814390867561894)
XLA Ops:
  7.2 2.0 %shard_map.131 = bf16[88,768]{1,0:T(8,128)(2,1)} custom-call(bf16[87,232]{1,0:T(8,128)(2,1)} %bitcast.26, bf16[87,384]{1,0:T(8,128)(2,1)} %project_in.1, f32[58,87]{1,0:T(8,128)} %bitcast.27, f32[58,87]{1,0:T(8,128)} %excite_in.1, f32[9,87]{1,0:T(8,128)} %depth_in.1), custom_call_target="tpu_custom_call" | custom-call | flops 1000000 | bytes 1000000 | tf_op jit(solution)/shard_map/pallas_call | solution.py:54
  9.3 1.8 %convolution_convert_fusion.1 = bf16[768,384]{1,0:T(8,128)(2,1)S(1)} fusion(bf16[768,512]{1,0:T(8,128)(2,1)} %param.23, bf16[384,512]{1,0:T(8,128)(2,1)} %param.22), kind=kOutput, calls=%fused_computation.1 | convolution fusion | flops 302284800 | bytes 1769472 | tf_op jit(solution)/shard_map/dot_general | solution.py:28
  11.1 28.2 %all_to_all.20 = bf16[32,24,384]{2,1,0:T(8,128)(2,1)S(1)} all-to-all(bf16[32,24,384]{2,1,0:T(8,128)(2,1)S(1)} %bitcast.23), channel_id=1, replica_groups=mesh['seq'=32,'mp'=16] {'seq'}, dimensions={0} | all-to-all | bytes 1179648 | tf_op jit(solution)/shard_map/all_to_all | solution.py:343
  39.3 1.4 %shard_map.132.after = bf16[16,24,384]{2,1,0:T(8,128)(2,1)} custom-call(bf16[768,384]{1,0:T(8,128)(2,1)S(1)} %bitcast.17, s32[1,384]{1,0:T(1,128)S(1)} %bitcast.21), custom_call_target="tpu_custom_call" | custom-call | flops 300000000 | bytes 2000000 | tf_op jit(solution)/shard_map/pallas_call | solution.py:54
  40.7 10.4 %all-to-all-start.2 = ((bf16[16,24,384]{2,1,0:T(8,128)(2,1)}), bf16[16,24,384]{2,1,0:T(8,128)(2,1)S(1)}, u32[]{:S(2)}, u32[]{:S(2)}) async-start(bf16[16,24,384]{2,1,0:T(8,128)(2,1)} %shard_map.132.after), calls=%async_computation.2 | async-start | bytes 589824 | tf_op jit(solution)/shard_map/all_to_all | solution.py:352
  52.2 7.9 %all-gather.2.cloned.1.call-done.packed = bf16[1408,768]{1,0:T(8,128)(2,1)} async-done(((bf16[88,768]{1,0:T(8,128)(2,1)}), bf16[1408,768]{1,0:T(8,128)(2,1)}) %all-gather.2.cloned.1.call-update) | async-done | bytes 2162704 | tf_op jit(solution)/shard_map/all_gather | solution.py:341
  60.1 8.1 %shard_map.133 = (bf16[16,24,384]{2,1,0:T(8,128)(2,1)}, f32[352,384]{1,0:T(8,128)}) custom-call(s32[48]{0:T(128)} %ids.1, bf16[320,256]{1,0:T(8,128)(2,1)} %bitcast.25, f32[64,2,384]{2,1,0:T(2,128)} %table.1, f32[8,384]{1,0:T(8,128)} %bitcast.19, bf16[1408,768]{1,0:T(8,128)(2,1)} %all-gather.2.cloned.1.call-done.packed, bf16[16,24,384]{2,1,0:T(8,128)(2,1)} %shard_map.132.after), custom_call_target="tpu_custom_call" | custom-call | flops 2000000000 | bytes 30000000 | tf_op jit(solution)/shard_map/pallas_call | solution.py:54
  68.2 4.2 %all-to-all-start.1 = ((bf16[16,24,384]{2,1,0:T(8,128)(2,1)}), bf16[16,24,384]{2,1,0:T(8,128)(2,1)S(1)}, u32[]{:S(2)}, u32[]{:S(2)}) async-start(bf16[16,24,384]{2,1,0:T(8,128)(2,1)} %get-tuple-element.13), calls=%async_computation.1 | async-start | bytes 589824 | tf_op jit(solution)/shard_map/all_to_all | solution.py:380
  72.4 1.0 copy-done.3
  73.4 1.7 %shard_map.134 = (bf16[4,24,384]{2,1,0:T(8,128)(2,1)S(1)}, bf16[4,24,384]{2,1,0:T(8,128)(2,1)S(1)}, bf16[4,24,384]{2,1,0:T(8,128)(2,1)S(1)}, bf16[4,24,384]{2,1,0:T(8,128)(2,1)S(1)}) custom-call(f32[352,384]{1,0:T(8,128)S(1)} %copy-done.3, f32[8,384]{1,0:T(8,128)S(1)} %bitcast.20, bf16[16,24,384]{2,1,0:T(8,128)(2,1)S(1)} %all-to-all-done.2.grads), custom_call_target="tpu_custom_call" | custom-call | flops 1000000000 | bytes 2000000 | tf_op jit(solution)/shard_map/pallas_call | solution.py:54
  75.2 4.7 %collective-permute-start = (bf16[4,24,384]{2,1,0:T(8,128)(2,1)S(1)}, bf16[4,24,384]{2,1,0:T(8,128)(2,1)S(1)}, u32[]{:S(2)}, u32[]{:S(2)}) collective-permute-start(bf16[4,24,384]{2,1,0:T(8,128)(2,1)S(1)} %get-tuple-element.15), channel_id=1, source_target_pairs={{0,4},{1,5},{2,6},{3,7},{4,0},{5,1},{6,2},{7,3},{8,12},{9,13},{10,... | collective-permute-start | bytes 221192 | tf_op jit(solution)/shard_map/ppermute | solution.py:392
  79.9 6.0 %collective-permute-done.after.refs_1_ = bf16[4,24,384]{2,1,0:T(8,128)(2,1)S(1)} collective-permute-done((bf16[4,24,384]{2,1,0:T(8,128)(2,1)S(1)}, bf16[4,24,384]{2,1,0:T(8,128)(2,1)S(1)}, u32[]{:S(2)}, u32[]{:S(2)}) %collective-permute-start) | collective-permute-done | bytes 73760 | tf_op jit(solution)/shard_map/ppermute | solution.py:392
  85.9 1.5 %shard_map.135.after = bf16[768,384]{1,0:T(8,128)(2,1)} custom-call(bf16[384,384]{1,0:T(8,128)(2,1)S(1)} %bitcast.18, s32[1,384]{1,0:T(1,128)S(1)} %bitcast.22, bf16[4,24,384]{2,1,0:T(8,128)(2,1)S(1)} %collective-permute-done.after.refs_1_), custom_call_target="tpu_custom_call" | custom-call | flops 300000000 | bytes 2000000 | tf_op jit(solution)/shard_map/pallas_call | solution.py:54
  87.4 10.9 %all-to-all-start.3 = ((bf16[32,24,384]{2,1,0:T(8,128)(2,1)}), bf16[32,24,384]{2,1,0:T(8,128)(2,1)}, u32[]{:S(2)}, u32[]{:S(2)}) async-start(bf16[32,24,384]{2,1,0:T(8,128)(2,1)} %bitcast.9), calls=%async_computation.3 | async-start | bytes 1179648 | tf_op jit(solution)/shard_map/all_to_all | solution.py:405
  98.3 5.7 %collective-permute-start.1 = (bf16[4,24,384]{2,1,0:T(8,128)(2,1)S(1)}, bf16[4,24,384]{2,1,0:T(8,128)(2,1)S(1)}, u32[]{:S(2)}, u32[]{:S(2)}) collective-permute-start(bf16[4,24,384]{2,1,0:T(8,128)(2,1)S(1)} %get-tuple-element.17), channel_id=1, source_target_pairs={{0,8},{1,9},{2,10},{3,11},{4,12},{5,13},{6,14},{7,15},{8,0},{9,1},... | collective-permute-start | bytes 221192 | tf_op jit(solution)/shard_map/ppermute | solution.py:392
  104.1 1.9 %collective-permute-start.2 = (bf16[4,24,384]{2,1,0:T(8,128)(2,1)S(1)}, bf16[4,24,384]{2,1,0:T(8,128)(2,1)S(1)}, u32[]{:S(2)}, u32[]{:S(2)}) collective-permute-start(bf16[4,24,384]{2,1,0:T(8,128)(2,1)S(1)} %get-tuple-element.18), channel_id=1, source_target_pairs={{0,12},{1,13},{2,14},{3,15},{4,8},{5,9},{6,10},{7,11},{8,4},{9,5},... | collective-permute-start | bytes 221192 | tf_op jit(solution)/shard_map/ppermute | solution.py:392
  106.0 3.1 %collective-permute-done.1.refs_2_ = bf16[4,24,384]{2,1,0:T(8,128)(2,1)S(1)} collective-permute-done((bf16[4,24,384]{2,1,0:T(8,128)(2,1)S(1)}, bf16[4,24,384]{2,1,0:T(8,128)(2,1)S(1)}, u32[]{:S(2)}, u32[]{:S(2)}) %collective-permute-start.1) | collective-permute-done | bytes 73760 | tf_op jit(solution)/shard_map/ppermute | solution.py:392
  109.1 3.3 %collective-permute-done.2.refs_3_ = bf16[4,24,384]{2,1,0:T(8,128)(2,1)S(1)} collective-permute-done((bf16[4,24,384]{2,1,0:T(8,128)(2,1)S(1)}, bf16[4,24,384]{2,1,0:T(8,128)(2,1)S(1)}, u32[]{:S(2)}, u32[]{:S(2)}) %collective-permute-start.2) | collective-permute-done | bytes 73760 | tf_op jit(solution)/shard_map/ppermute | solution.py:392
  112.5 1.9 %collective-permute-start.3 = (bf16[4,24,384]{2,1,0:T(8,128)(2,1)S(1)}, bf16[4,24,384]{2,1,0:T(8,128)(2,1)S(1)}, u32[]{:S(2)}, u32[]{:S(2)}) collective-permute-start(bf16[4,24,384]{2,1,0:T(8,128)(2,1)S(1)} %get-tuple-element.19), channel_id=1, source_target_pairs={{0,1},{1,0},{2,3},{3,2},{4,5},{5,4},{6,7},{7,6},{8,9},{9,8},{10,11... | collective-permute-start | bytes 221192 | tf_op jit(solution)/shard_map/ppermute | solution.py:392
  114.4 2.0 %collective-permute-start.4 = (bf16[4,24,384]{2,1,0:T(8,128)(2,1)S(1)}, bf16[4,24,384]{2,1,0:T(8,128)(2,1)S(1)}, u32[]{:S(2)}, u32[]{:S(2)}) collective-permute-start(bf16[4,24,384]{2,1,0:T(8,128)(2,1)S(1)} %get-tuple-element.20), channel_id=1, source_target_pairs={{0,2},{1,3},{2,0},{3,1},{4,6},{5,7},{6,4},{7,5},{8,10},{9,11},{10,... | collective-permute-start | bytes 221192 | tf_op jit(solution)/shard_map/ppermute | solution.py:392
  116.4 3.7 %collective-permute-start.5 = (bf16[4,24,384]{2,1,0:T(8,128)(2,1)S(1)}, bf16[4,24,384]{2,1,0:T(8,128)(2,1)S(1)}, u32[]{:S(2)}, u32[]{:S(2)}) collective-permute-start(bf16[4,24,384]{2,1,0:T(8,128)(2,1)S(1)} %get-tuple-element.21), channel_id=1, source_target_pairs={{0,3},{1,2},{2,1},{3,0},{4,7},{5,6},{6,5},{7,4},{8,11},{9,10},{10,... | collective-permute-start | bytes 221192 | tf_op jit(solution)/shard_map/ppermute | solution.py:392
  120.1 0.9 collective-permute-done.4.refs_5_
  120.9 1.4 %collective-permute-done.5.refs_6_ = bf16[4,24,384]{2,1,0:T(8,128)(2,1)S(1)} collective-permute-done((bf16[4,24,384]{2,1,0:T(8,128)(2,1)S(1)}, bf16[4,24,384]{2,1,0:T(8,128)(2,1)S(1)}, u32[]{:S(2)}, u32[]{:S(2)}) %collective-permute-start.5) | collective-permute-done | bytes 73760 | tf_op jit(solution)/shard_map/ppermute | solution.py:392
  123.1 2.6 %convolution_convert_fusion = bf16[768,512]{1,0:T(8,128)(2,1)} fusion(bf16[768,384]{1,0:T(8,128)(2,1)} %bitcast.10, bf16[384,512]{1,0:T(8,128)(2,1)} %param.22), kind=kOutput, calls=%fused_computation | convolution fusion | flops 302383104 | bytes 1769472 | tf_op jit(solution)/shard_map/dot_general | solution.py:28
  (18 shorter events, 1.9 us)
Async XLA Ops:
  7.2 44.0 %copy-start = (bf16[48,100,232]{2,0,1:T(8,128)(2,1)S(1)}, bf16[48,100,232]{2,0,1:T(8,128)(2,1)}, u32[]{:S(2)}) copy-start(bf16[48,100,232]{2,0,1:T(8,128)(2,1)} %param.12) | copy-start | bytes 6681604
  7.2 32.2 %copy-start.2 = (s32[384,1]{0,1:T(1,128)S(1)}, s32[384,1]{0,1:T(1,128)}, u32[]{:S(2)}) copy-start(s32[384,1]{0,1:T(1,128)} %param.21) | copy-start | bytes 4612
  7.2 52.9 %all-gather.2.cloned.1.call-start = ((), (), s32[]{:S(2)}) async-start(), calls=%async_computation.4 | async-start | bytes 2297856 | tf_op jit(solution)/shard_map/all_gather | solution.py:341
  40.7 27.4 %all-to-all-start.2 = ((bf16[16,24,384]{2,1,0:T(8,128)(2,1)}), bf16[16,24,384]{2,1,0:T(8,128)(2,1)S(1)}, u32[]{:S(2)}, u32[]{:S(2)}) async-start(bf16[16,24,384]{2,1,0:T(8,128)(2,1)} %shard_map.132.after), calls=%async_computation.2 | async-start | bytes 589824 | tf_op jit(solution)/shard_map/all_to_all | solution.py:352
  60.1 12.3 %copy-start.1 = (f32[384,8]{0,1:T(8,128)S(1)}, f32[384,8]{0,1:T(8,128)}, u32[]{:S(2)}) copy-start(f32[384,8]{0,1:T(8,128)} %param.20) | copy-start | bytes 36868
  68.2 17.7 %all-to-all-start.1 = ((bf16[16,24,384]{2,1,0:T(8,128)(2,1)}), bf16[16,24,384]{2,1,0:T(8,128)(2,1)S(1)}, u32[]{:S(2)}, u32[]{:S(2)}) async-start(bf16[16,24,384]{2,1,0:T(8,128)(2,1)} %get-tuple-element.13), calls=%async_computation.1 | async-start | bytes 589824 | tf_op jit(solution)/shard_map/all_to_all | solution.py:380
  72.4 1.1 copy-start.3
  75.2 10.7 %collective-permute-start = (bf16[4,24,384]{2,1,0:T(8,128)(2,1)S(1)}, bf16[4,24,384]{2,1,0:T(8,128)(2,1)S(1)}, u32[]{:S(2)}, u32[]{:S(2)}) collective-permute-start(bf16[4,24,384]{2,1,0:T(8,128)(2,1)S(1)} %get-tuple-element.15), channel_id=1, source_target_pairs={{0,4},{1,5},{2,6},{3,7},{4,0},{5,1},{6,2},{7,3},{8,12},{9,13},{10,... | collective-permute-start | bytes 221192 | tf_op jit(solution)/shard_map/ppermute | solution.py:392
  87.4 35.7 %all-to-all-start.3 = ((bf16[32,24,384]{2,1,0:T(8,128)(2,1)}), bf16[32,24,384]{2,1,0:T(8,128)(2,1)}, u32[]{:S(2)}, u32[]{:S(2)}) async-start(bf16[32,24,384]{2,1,0:T(8,128)(2,1)} %bitcast.9), calls=%async_computation.3 | async-start | bytes 1179648 | tf_op jit(solution)/shard_map/all_to_all | solution.py:405
  98.3 10.8 %collective-permute-start.1 = (bf16[4,24,384]{2,1,0:T(8,128)(2,1)S(1)}, bf16[4,24,384]{2,1,0:T(8,128)(2,1)S(1)}, u32[]{:S(2)}, u32[]{:S(2)}) collective-permute-start(bf16[4,24,384]{2,1,0:T(8,128)(2,1)S(1)} %get-tuple-element.17), channel_id=1, source_target_pairs={{0,8},{1,9},{2,10},{3,11},{4,12},{5,13},{6,14},{7,15},{8,0},{9,1},... | collective-permute-start | bytes 221192 | tf_op jit(solution)/shard_map/ppermute | solution.py:392
  104.1 8.4 %collective-permute-start.2 = (bf16[4,24,384]{2,1,0:T(8,128)(2,1)S(1)}, bf16[4,24,384]{2,1,0:T(8,128)(2,1)S(1)}, u32[]{:S(2)}, u32[]{:S(2)}) collective-permute-start(bf16[4,24,384]{2,1,0:T(8,128)(2,1)S(1)} %get-tuple-element.18), channel_id=1, source_target_pairs={{0,12},{1,13},{2,14},{3,15},{4,8},{5,9},{6,10},{7,11},{8,4},{9,5},... | collective-permute-start | bytes 221192 | tf_op jit(solution)/shard_map/ppermute | solution.py:392
  112.5 7.6 %collective-permute-start.3 = (bf16[4,24,384]{2,1,0:T(8,128)(2,1)S(1)}, bf16[4,24,384]{2,1,0:T(8,128)(2,1)S(1)}, u32[]{:S(2)}, u32[]{:S(2)}) collective-permute-start(bf16[4,24,384]{2,1,0:T(8,128)(2,1)S(1)} %get-tuple-element.19), channel_id=1, source_target_pairs={{0,1},{1,0},{2,3},{3,2},{4,5},{5,4},{6,7},{7,6},{8,9},{9,8},{10,11... | collective-permute-start | bytes 221192 | tf_op jit(solution)/shard_map/ppermute | solution.py:392
  114.4 6.6 %collective-permute-start.4 = (bf16[4,24,384]{2,1,0:T(8,128)(2,1)S(1)}, bf16[4,24,384]{2,1,0:T(8,128)(2,1)S(1)}, u32[]{:S(2)}, u32[]{:S(2)}) collective-permute-start(bf16[4,24,384]{2,1,0:T(8,128)(2,1)S(1)} %get-tuple-element.20), channel_id=1, source_target_pairs={{0,2},{1,3},{2,0},{3,1},{4,6},{5,7},{6,4},{7,5},{8,10},{9,11},{10,... | collective-permute-start | bytes 221192 | tf_op jit(solution)/shard_map/ppermute | solution.py:392
  116.4 6.0 %collective-permute-start.5 = (bf16[4,24,384]{2,1,0:T(8,128)(2,1)S(1)}, bf16[4,24,384]{2,1,0:T(8,128)(2,1)S(1)}, u32[]{:S(2)}, u32[]{:S(2)}) collective-permute-start(bf16[4,24,384]{2,1,0:T(8,128)(2,1)S(1)} %get-tuple-element.21), channel_id=1, source_target_pairs={{0,3},{1,2},{2,1},{3,0},{4,7},{5,6},{6,5},{7,4},{8,11},{9,10},{10,... | collective-permute-start | bytes 221192 | tf_op jit(solution)/shard_map/ppermute | solution.py:392
Sparse Core Ops, SparseCore 0:
  10.7 49.2 all-gather.1

commit v6 on v5

--- a/solution.py
+++ b/solution.py
@@ -281,6 +281,14 @@
             out[k] = part[j + 1]
 
 
+def project_kernel(rows, weights, after, out):
+    del after
+    step = rows.shape[0] // 3
+    for k in range(3):
+        band = slice(k * step, (k + 1) * step)
+        out[band, :] = dot(rows[band, :], weights[...]).astype(bf16)
+
+
 def settle_kernel(*refs):
     *parts, out = refs
     n_frames = 3
@@ -401,14 +409,19 @@
     )
     joined = call(join_kernel, (blocks,) * (near - 1), outgoing, *parts,
                   in_specs=[pl.BlockSpec(memory_space=pl.ANY)] + [vmem] * len(parts))
+    ready = joined[0]
     joined = [swap(part, j + 1) for j, part in enumerate(joined)]
     rows_in = lax.all_to_all(
         outgoing.reshape(peers, capacity, width), "seq", split_axis=0, concat_axis=0, tiled=True
     )
     feature_grad = call(settle_kernel, sds((count, share, cells), bf16), *parts, *joined)
-    rows_in, feature_grad = lax.optimization_barrier((rows_in, feature_grad))
-    policy_in = dot(rows_in.reshape(peers * capacity, width), w_policy).astype(bf16)
-
+    policy_in = call(
+        project_kernel,
+        sds((peers * capacity, w_policy.shape[1]), bf16),
+        rows_in.reshape(peers * capacity, width), w_policy, ready,
+        in_specs=[vmem, vmem, pl.BlockSpec(memory_space=pl.ANY)],
+        flops=3e8, moved=2e6,
+    )
     feature_grad = feature_grad.transpose(0, 2, 1)
     return (policy_in, feature_grad)
 

time: 135 us -> 138 us (1.022)
  local copies, waits for them, and re-layouts: 2.04 us -> 7.54 us
  matrix products: 4.44 us -> 1.82 us
    unnamed x8 -> x26, local copies, waits for them, and re-layouts: 1.06 us -> 6.56 us
    dot_general x2 -> x1, matrix products: 4.44 us -> 1.82 us  [dot(): lax.dot_general(a, b, dims, precision=precision, preferred_element_type=f32)]
    pallas_call x7 -> x8, Pallas kernels: 15.5 us -> 16.1 us  [call(): pl.pallas_call(kernel, out_shape=out_shape, in_specs=in_specs or [pl.Bloc...]
where the time goes in v6:
time: 138 us; the launch traced here: 136 us
  starting transfers between devices  46.6 us (34%)
  blocking collectives  28.2 us (20%)
  waiting for transfers between devices  21.8 us (16%)
  Pallas kernels  16.1 us (12%)
  between operations  14.2 us (10%)
  local copies, waits for them, and re-layouts  7.54 us (5%)
  matrix products  1.82 us (1%)
    all_to_all x1, blocking collectives, per_device(): lax.all_to_all(grad_part.reshape(peers, capacity, width), 'seq', split_ax...  28.2 us
    ppermute x6, starting transfers between devices, swap(): lax.ppermute(value, 'mp', [(m, m ^ far) for m in range(n_mp)])  21 us
    pallas_call x8, Pallas kernels, call(): pl.pallas_call(kernel, out_shape=out_shape, in_specs=in_specs or [pl.Bloc...  16.1 us
    ppermute x6, waiting for transfers between devices, swap(): lax.ppermute(value, 'mp', [(m, m ^ far) for m in range(n_mp)])  13.9 us
    all_to_all x1, starting transfers between devices, per_device(): lax.all_to_all(outgoing.reshape(peers, capacity, width), 'seq', split_axi...  10.9 us
    all_to_all x1, starting transfers between devices, per_device(): lax.all_to_all(picked, 'mp', split_axis=0, concat_axis=0, tiled=True)  10.4 us
    all_gather x1, waiting for transfers between devices, per_device(): packed = lax.all_gather(mine, 'mp', axis=0, tiled=True)  7.9 us
    unnamed x26, local copies, waits for them, and re-layouts  6.56 us
  transfers between devices with their start and end apart: 10, of which 6 were waited for; matrix products, arithmetic and copies ran while one was open for 2% of the time, Pallas kernels for 9%

profile of v6, /device:TPU:6, one launch (start us, length us, event | category | flops | bytes accessed | tf_op | source)
XLA Modules:
  0.0 136.4 jit_solution(2481912937521366154)
XLA Ops:
  7.2 2.0 %shard_map.131 = bf16[88,768]{1,0:T(8,128)(2,1)} custom-call(bf16[87,232]{1,0:T(8,128)(2,1)} %bitcast.26, bf16[87,384]{1,0:T(8,128)(2,1)} %project_in.1, f32[58,87]{1,0:T(8,128)} %bitcast.27, f32[58,87]{1,0:T(8,128)} %excite_in.1, f32[9,87]{1,0:T(8,128)} %depth_in.1), custom_call_target="tpu_custom_call" | custom-call | flops 1000000 | bytes 1000000 | tf_op jit(solution)/shard_map/pallas_call | solution.py:54
  9.3 1.8 %convolution_convert_fusion = bf16[768,384]{1,0:T(8,128)(2,1)S(1)} fusion(bf16[768,512]{1,0:T(8,128)(2,1)} %param.23, bf16[384,512]{1,0:T(8,128)(2,1)} %weights.1), kind=kOutput, calls=%fused_computation | convolution fusion | flops 302284800 | bytes 1769472 | tf_op jit(solution)/shard_map/dot_general | solution.py:28
  11.1 28.2 %all_to_all.20 = bf16[32,24,384]{2,1,0:T(8,128)(2,1)S(1)} all-to-all(bf16[32,24,384]{2,1,0:T(8,128)(2,1)S(1)} %bitcast.23), channel_id=1, replica_groups=mesh['seq'=32,'mp'=16] {'seq'}, dimensions={0} | all-to-all | bytes 1179648 | tf_op jit(solution)/shard_map/all_to_all | solution.py:351
  39.3 1.4 %shard_map.132.after = bf16[16,24,384]{2,1,0:T(8,128)(2,1)} custom-call(bf16[768,384]{1,0:T(8,128)(2,1)S(1)} %bitcast.17, s32[1,384]{1,0:T(1,128)S(1)} %bitcast.21), custom_call_target="tpu_custom_call" | custom-call | flops 300000000 | bytes 2000000 | tf_op jit(solution)/shard_map/pallas_call | solution.py:54
  40.7 10.4 %all-to-all-start.2 = ((bf16[16,24,384]{2,1,0:T(8,128)(2,1)}), bf16[16,24,384]{2,1,0:T(8,128)(2,1)S(1)}, u32[]{:S(2)}, u32[]{:S(2)}) async-start(bf16[16,24,384]{2,1,0:T(8,128)(2,1)} %shard_map.132.after), calls=%async_computation.2 | async-start | bytes 589824 | tf_op jit(solution)/shard_map/all_to_all | solution.py:360
  52.2 7.9 %all-gather.2.cloned.1.call-done.packed = bf16[1408,768]{1,0:T(8,128)(2,1)} async-done(((bf16[88,768]{1,0:T(8,128)(2,1)}), bf16[1408,768]{1,0:T(8,128)(2,1)}) %all-gather.2.cloned.1.call-update) | async-done | bytes 2162704 | tf_op jit(solution)/shard_map/all_gather | solution.py:349
  60.1 8.1 %shard_map.133 = (bf16[16,24,384]{2,1,0:T(8,128)(2,1)}, f32[352,384]{1,0:T(8,128)}) custom-call(s32[48]{0:T(128)} %ids.1, bf16[320,256]{1,0:T(8,128)(2,1)} %bitcast.25, f32[64,2,384]{2,1,0:T(2,128)} %table.1, f32[8,384]{1,0:T(8,128)} %bitcast.19, bf16[1408,768]{1,0:T(8,128)(2,1)} %all-gather.2.cloned.1.call-done.packed, bf16[16,24,384]{2,1,0:T(8,128)(2,1)} %shard_map.132.after), custom_call_target="tpu_custom_call" | custom-call | flops 2000000000 | bytes 30000000 | tf_op jit(solution)/shard_map/pallas_call | solution.py:54
  68.1 4.2 %all-to-all-start.1 = ((bf16[16,24,384]{2,1,0:T(8,128)(2,1)}), bf16[16,24,384]{2,1,0:T(8,128)(2,1)S(1)}, u32[]{:S(2)}, u32[]{:S(2)}) async-start(bf16[16,24,384]{2,1,0:T(8,128)(2,1)} %get-tuple-element.11), calls=%async_computation.1 | async-start | bytes 589824 | tf_op jit(solution)/shard_map/all_to_all | solution.py:388
  72.4 1.0 copy-done.12
  73.4 1.7 %shard_map.134 = (bf16[4,24,384]{2,1,0:T(8,128)(2,1)S(1)}, bf16[4,24,384]{2,1,0:T(8,128)(2,1)S(1)}, bf16[4,24,384]{2,1,0:T(8,128)(2,1)S(1)}, bf16[4,24,384]{2,1,0:T(8,128)(2,1)S(1)}) custom-call(f32[352,384]{1,0:T(8,128)S(1)} %copy-done.12, f32[8,384]{1,0:T(8,128)S(1)} %bitcast.20, bf16[16,24,384]{2,1,0:T(8,128)(2,1)S(1)} %all-to-all-done.2.grads), custom_call_target="tpu_custom_call" | custom-call | flops 1000000000 | bytes 2000000 | tf_op jit(solution)/shard_map/pallas_call | solution.py:54
  76.4 4.8 %collective-permute-start = (bf16[4,24,384]{2,1,0:T(8,128)(2,1)S(1)}, bf16[4,24,384]{2,1,0:T(8,128)(2,1)S(1)}, u32[]{:S(2)}, u32[]{:S(2)}) collective-permute-start(bf16[4,24,384]{2,1,0:T(8,128)(2,1)S(1)} %get-tuple-element.13), channel_id=1, source_target_pairs={{0,4},{1,5},{2,6},{3,7},{4,0},{5,1},{6,2},{7,3},{8,12},{9,13},{10,... | collective-permute-start | bytes 221192 | tf_op jit(solution)/shard_map/ppermute | solution.py:400
  81.3 5.0 %collective-permute-done.after.refs_1_ = bf16[4,24,384]{2,1,0:T(8,128)(2,1)S(1)} collective-permute-done((bf16[4,24,384]{2,1,0:T(8,128)(2,1)S(1)}, bf16[4,24,384]{2,1,0:T(8,128)(2,1)S(1)}, u32[]{:S(2)}, u32[]{:S(2)}) %collective-permute-start) | collective-permute-done | bytes 73760 | tf_op jit(solution)/shard_map/ppermute | solution.py:400
  87.8 10.9 %all-to-all-start.3 = ((bf16[32,24,384]{2,1,0:T(8,128)(2,1)}), bf16[32,24,384]{2,1,0:T(8,128)(2,1)S(1)}, u32[]{:S(2)}, u32[]{:S(2)}) async-start(bf16[32,24,384]{2,1,0:T(8,128)(2,1)} %bitcast.16), calls=%async_computation.3 | async-start | bytes 1179648 | tf_op jit(solution)/shard_map/all_to_all | solution.py:414
  98.7 6.7 %collective-permute-start.1 = (bf16[4,24,384]{2,1,0:T(8,128)(2,1)}, bf16[4,24,384]{2,1,0:T(8,128)(2,1)S(1)}, u32[]{:S(2)}, u32[]{:S(2)}) collective-permute-start(bf16[4,24,384]{2,1,0:T(8,128)(2,1)} %copy-done.9), channel_id=1, source_target_pairs={{0,8},{1,9},{2,10},{3,11},{4,12},{5,13},{6,14},{7,15},{8,0},{9,1},... | collective-permute-start | bytes 221192 | tf_op jit(solution)/shard_map/ppermute | solution.py:400
  105.4 1.9 %collective-permute-start.2 = (bf16[4,24,384]{2,1,0:T(8,128)(2,1)}, bf16[4,24,384]{2,1,0:T(8,128)(2,1)S(1)}, u32[]{:S(2)}, u32[]{:S(2)}) collective-permute-start(bf16[4,24,384]{2,1,0:T(8,128)(2,1)} %copy-done.8), channel_id=1, source_target_pairs={{0,12},{1,13},{2,14},{3,15},{4,8},{5,9},{6,10},{7,11},{8,4},{9,5},... | collective-permute-start | bytes 221192 | tf_op jit(solution)/shard_map/ppermute | solution.py:400
  107.3 2.5 %collective-permute-done.1.refs_2_ = bf16[4,24,384]{2,1,0:T(8,128)(2,1)S(1)} collective-permute-done((bf16[4,24,384]{2,1,0:T(8,128)(2,1)}, bf16[4,24,384]{2,1,0:T(8,128)(2,1)S(1)}, u32[]{:S(2)}, u32[]{:S(2)}) %collective-permute-start.1) | collective-permute-done | bytes 73760 | tf_op jit(solution)/shard_map/ppermute | solution.py:400
  109.8 4.1 %collective-permute-done.2.refs_3_ = bf16[4,24,384]{2,1,0:T(8,128)(2,1)S(1)} collective-permute-done((bf16[4,24,384]{2,1,0:T(8,128)(2,1)}, bf16[4,24,384]{2,1,0:T(8,128)(2,1)S(1)}, u32[]{:S(2)}, u32[]{:S(2)}) %collective-permute-start.2) | collective-permute-done | bytes 73760 | tf_op jit(solution)/shard_map/ppermute | solution.py:400
  114.0 1.1 copy-done.2
  115.9 1.9 %collective-permute-start.3 = (bf16[4,24,384]{2,1,0:T(8,128)(2,1)S(1)}, bf16[4,24,384]{2,1,0:T(8,128)(2,1)S(1)}, u32[]{:S(2)}, u32[]{:S(2)}) collective-permute-start(bf16[4,24,384]{2,1,0:T(8,128)(2,1)S(1)} %get-tuple-element.17.after), channel_id=1, source_target_pairs={{0,1},{1,0},{2,3},{3,2},{4,5},{5,4},{6,7},{7,6},{8,9},{9,8},{10,11... | collective-permute-start | bytes 221192 | tf_op jit(solution)/shard_map/ppermute | solution.py:400
  118.5 1.9 %collective-permute-start.4 = (bf16[4,24,384]{2,1,0:T(8,128)(2,1)S(1)}, bf16[4,24,384]{2,1,0:T(8,128)(2,1)S(1)}, u32[]{:S(2)}, u32[]{:S(2)}) collective-permute-start(bf16[4,24,384]{2,1,0:T(8,128)(2,1)S(1)} %get-tuple-element.18), channel_id=1, source_target_pairs={{0,2},{1,3},{2,0},{3,1},{4,6},{5,7},{6,4},{7,5},{8,10},{9,11},{10,... | collective-permute-start | bytes 221192 | tf_op jit(solution)/shard_map/ppermute | solution.py:400
  120.4 3.7 %collective-permute-start.5 = (bf16[4,24,384]{2,1,0:T(8,128)(2,1)S(1)}, bf16[4,24,384]{2,1,0:T(8,128)(2,1)S(1)}, u32[]{:S(2)}, u32[]{:S(2)}) collective-permute-start(bf16[4,24,384]{2,1,0:T(8,128)(2,1)S(1)} %get-tuple-element.19), channel_id=1, source_target_pairs={{0,3},{1,2},{2,1},{3,0},{4,7},{5,6},{6,5},{7,4},{8,11},{9,10},{10,... | collective-permute-start | bytes 221192 | tf_op jit(solution)/shard_map/ppermute | solution.py:400
  125.0 1.4 %collective-permute-done.5.refs_6_ = bf16[4,24,384]{2,1,0:T(8,128)(2,1)S(1)} collective-permute-done((bf16[4,24,384]{2,1,0:T(8,128)(2,1)S(1)}, bf16[4,24,384]{2,1,0:T(8,128)(2,1)S(1)}, u32[]{:S(2)}, u32[]{:S(2)}) %collective-permute-start.5) | collective-permute-done | bytes 73760 | tf_op jit(solution)/shard_map/ppermute | solution.py:400
  127.2 0.9 copy-done.7
  128.1 1.4 %shard_map.137 = bf16[768,512]{1,0:T(8,128)(2,1)} custom-call(bf16[768,384]{1,0:T(8,128)(2,1)S(1)} %bitcast.15, bf16[384,512]{1,0:T(8,128)(2,1)S(1)} %copy-done.3, bf16[4,24,384]{2,1,0:T(8,128)(2,1)S(1)} %copy-done.7), custom_call_target="tpu_custom_call" | custom-call | flops 300000000 | bytes 2000000 | tf_op jit(solution)/shard_map/pallas_call | solution.py:54
  (36 shorter events, 7.0 us)
Async XLA Ops:
  7.2 44.0 %copy-start = (bf16[48,100,232]{2,0,1:T(8,128)(2,1)S(1)}, bf16[48,100,232]{2,0,1:T(8,128)(2,1)}, u32[]{:S(2)}) copy-start(bf16[48,100,232]{2,0,1:T(8,128)(2,1)} %param.12) | copy-start | bytes 6681604
  7.2 32.2 %copy-start.11 = (s32[384,1]{0,1:T(1,128)S(1)}, s32[384,1]{0,1:T(1,128)}, u32[]{:S(2)}) copy-start(s32[384,1]{0,1:T(1,128)} %param.21) | copy-start | bytes 4612
  7.2 52.9 %all-gather.2.cloned.1.call-start = ((), (), s32[]{:S(2)}) async-start(), calls=%async_computation.4 | async-start | bytes 2297856 | tf_op jit(solution)/shard_map/all_gather | solution.py:349
  40.7 27.4 %all-to-all-start.2 = ((bf16[16,24,384]{2,1,0:T(8,128)(2,1)}), bf16[16,24,384]{2,1,0:T(8,128)(2,1)S(1)}, u32[]{:S(2)}, u32[]{:S(2)}) async-start(bf16[16,24,384]{2,1,0:T(8,128)(2,1)} %shard_map.132.after), calls=%async_computation.2 | async-start | bytes 589824 | tf_op jit(solution)/shard_map/all_to_all | solution.py:360
  60.1 12.3 %copy-start.10 = (f32[384,8]{0,1:T(8,128)S(1)}, f32[384,8]{0,1:T(8,128)}, u32[]{:S(2)}) copy-start(f32[384,8]{0,1:T(8,128)} %param.20) | copy-start | bytes 36868
  68.1 18.1 %all-to-all-start.1 = ((bf16[16,24,384]{2,1,0:T(8,128)(2,1)}), bf16[16,24,384]{2,1,0:T(8,128)(2,1)S(1)}, u32[]{:S(2)}, u32[]{:S(2)}) async-start(bf16[16,24,384]{2,1,0:T(8,128)(2,1)} %get-tuple-element.11), calls=%async_computation.1 | async-start | bytes 589824 | tf_op jit(solution)/shard_map/all_to_all | solution.py:388
  72.4 1.1 copy-start.12
  75.2 0.6 copy-start.8
  75.8 0.6 copy-start.9
  76.4 50.8 %copy-start.3 = (bf16[384,512]{1,0:T(8,128)(2,1)S(1)}, bf16[384,512]{1,0:T(8,128)(2,1)}, u32[]{:S(2)}) copy-start(bf16[384,512]{1,0:T(8,128)(2,1)} %weights.1) | copy-start | bytes 1179652
  76.4 9.9 %collective-permute-start = (bf16[4,24,384]{2,1,0:T(8,128)(2,1)S(1)}, bf16[4,24,384]{2,1,0:T(8,128)(2,1)S(1)}, u32[]{:S(2)}, u32[]{:S(2)}) collective-permute-start(bf16[4,24,384]{2,1,0:T(8,128)(2,1)S(1)} %get-tuple-element.13), channel_id=1, source_target_pairs={{0,4},{1,5},{2,6},{3,7},{4,0},{5,1},{6,2},{7,3},{8,12},{9,13},{10,... | collective-permute-start | bytes 221192 | tf_op jit(solution)/shard_map/ppermute | solution.py:400
  86.3 1.5 %copy-start.4 = (bf16[4,24,384]{2,1,0:T(8,128)(2,1)}, bf16[4,24,384]{2,1,0:T(8,128)(2,1)S(1)}, u32[]{:S(2)}) copy-start(bf16[4,24,384]{2,1,0:T(8,128)(2,1)S(1)} %collective-permute-done.after.refs_1_) | copy-start | bytes 221188
  87.0 0.8 copy-start.1
  87.8 39.4 %all-to-all-start.3 = ((bf16[32,24,384]{2,1,0:T(8,128)(2,1)}), bf16[32,24,384]{2,1,0:T(8,128)(2,1)S(1)}, u32[]{:S(2)}, u32[]{:S(2)}) async-start(bf16[32,24,384]{2,1,0:T(8,128)(2,1)} %bitcast.16), calls=%async_computation.3 | async-start | bytes 1179648 | tf_op jit(solution)/shard_map/all_to_all | solution.py:414
  98.7 11.2 %collective-permute-start.1 = (bf16[4,24,384]{2,1,0:T(8,128)(2,1)}, bf16[4,24,384]{2,1,0:T(8,128)(2,1)S(1)}, u32[]{:S(2)}, u32[]{:S(2)}) collective-permute-start(bf16[4,24,384]{2,1,0:T(8,128)(2,1)} %copy-done.9), channel_id=1, source_target_pairs={{0,8},{1,9},{2,10},{3,11},{4,12},{5,13},{6,14},{7,15},{8,0},{9,1},... | collective-permute-start | bytes 221192 | tf_op jit(solution)/shard_map/ppermute | solution.py:400
  105.4 8.6 %collective-permute-start.2 = (bf16[4,24,384]{2,1,0:T(8,128)(2,1)}, bf16[4,24,384]{2,1,0:T(8,128)(2,1)S(1)}, u32[]{:S(2)}, u32[]{:S(2)}) collective-permute-start(bf16[4,24,384]{2,1,0:T(8,128)(2,1)} %copy-done.8), channel_id=1, source_target_pairs={{0,12},{1,13},{2,14},{3,15},{4,8},{5,9},{6,10},{7,11},{8,4},{9,5},... | collective-permute-start | bytes 221192 | tf_op jit(solution)/shard_map/ppermute | solution.py:400
  114.0 1.1 copy-start.2
  115.0 0.9 copy-start.5
  115.9 8.2 %collective-permute-start.3 = (bf16[4,24,384]{2,1,0:T(8,128)(2,1)S(1)}, bf16[4,24,384]{2,1,0:T(8,128)(2,1)S(1)}, u32[]{:S(2)}, u32[]{:S(2)}) collective-permute-start(bf16[4,24,384]{2,1,0:T(8,128)(2,1)S(1)} %get-tuple-element.17.after), channel_id=1, source_target_pairs={{0,1},{1,0},{2,3},{3,2},{4,5},{5,4},{6,7},{7,6},{8,9},{9,8},{10,11... | collective-permute-start | bytes 221192 | tf_op jit(solution)/shard_map/ppermute | solution.py:400
  117.9 0.6 copy-start.6
  118.5 6.6 %collective-permute-start.4 = (bf16[4,24,384]{2,1,0:T(8,128)(2,1)S(1)}, bf16[4,24,384]{2,1,0:T(8,128)(2,1)S(1)}, u32[]{:S(2)}, u32[]{:S(2)}) collective-permute-start(bf16[4,24,384]{2,1,0:T(8,128)(2,1)S(1)} %get-tuple-element.18), channel_id=1, source_target_pairs={{0,2},{1,3},{2,0},{3,1},{4,6},{5,7},{6,4},{7,5},{8,10},{9,11},{10,... | collective-permute-start | bytes 221192 | tf_op jit(solution)/shard_map/ppermute | solution.py:400
  120.4 6.0 %collective-permute-start.5 = (bf16[4,24,384]{2,1,0:T(8,128)(2,1)S(1)}, bf16[4,24,384]{2,1,0:T(8,128)(2,1)S(1)}, u32[]{:S(2)}, u32[]{:S(2)}) collective-permute-start(bf16[4,24,384]{2,1,0:T(8,128)(2,1)S(1)} %get-tuple-element.19), channel_id=1, source_target_pairs={{0,3},{1,2},{2,1},{3,0},{4,7},{5,6},{6,5},{7,4},{8,11},{9,10},{10,... | collective-permute-start | bytes 221192 | tf_op jit(solution)/shard_map/ppermute | solution.py:400
  127.2 0.9 copy-start.7
Sparse Core Ops, SparseCore 0:
  10.7 49.2 all-gather.1
